TPU v7x, 128 devices: a whole 4x4x4 slice. The times are simulated.
128 devices in a mesh: gx: 8 (over x_hi, z), gy: 16 (over y, x_lo, core).
Axes of the slice: x: 4 (x_hi: 2, x_lo: 2; x = x_hi * 2 + x_lo), y: 4, z: 4, core: 2. Of those that a mesh axis runs over, the one named last changes fastest.
Arguments:
- weights: bfloat16 [2097152, 128], P(('gx', 'gy')), may hold values from -6 to 6
- travel: float32 [2097152, 64], P(('gx', 'gy')), may hold values from -3.140625 to 3.140625
- interp_real: bfloat16 [8, 2, 2, 64, 64], replicated, may hold values from -0.375 to 0.375
- interp_imag: bfloat16 [8, 2, 2, 64, 64], replicated, may hold values from -0.375 to 0.375
- eval_real: bfloat16 [64, 64], replicated, may hold values from -0.5 to 0.5
- eval_imag: bfloat16 [64, 64], replicated, may hold values from -0.5 to 0.5
Outputs:
- image: bfloat16 [2097152, 128], P(('gx', 'gy'))
All inputs are finite; a program needn't handle non-finite values.
Results may differ from a plain program's by a relative error of at most 0.013.
Values may be sent and summed in bfloat16 or wider, within the bound.
A program may use at most 128 MiB of HBM per device.

v0:
```python
import jax
import jax.numpy as jnp
from jax import lax
from jax.sharding import PartitionSpec as P

LEVELS = 8


def from_partner(x, axis, stride):
    return lax.ppermute(x, axis, [(i, i ^ 1 << stride) for i in range(lax.axis_size(axis))])


def complex_block(part_real, part_imag):
    real_t = part_real.T
    imag_t = part_imag.T
    upper = jnp.concatenate([real_t, imag_t], 1)
    lower = jnp.concatenate([-imag_t, real_t], 1)
    return jnp.concatenate([upper, lower], 0)


def level_matrix(part_real, part_imag):
    row_blocks = []
    for c_in in range(2):
        col_blocks = []
        for c_out in range(2):
            col_blocks.append(complex_block(part_real[c_out, c_in], part_imag[c_out, c_in]))
        row_blocks.append(jnp.concatenate(col_blocks, 1))
    return jnp.concatenate(row_blocks, 0)


def rotate(values, angle):
    width = angle.shape[-1]
    real_part = values[..., :width]
    imag_part = values[..., width:]
    cosine = jnp.cos(angle)
    sine = jnp.sin(angle)
    return jnp.concatenate(
        [real_part * cosine - imag_part * sine, real_part * sine + imag_part * cosine], -1
    )


def local(weights, travel, interp_real, interp_imag, eval_real, eval_imag):
    pair_rows = weights.shape[0]
    width = weights.shape[1]
    half_rows = pair_rows // 2
    size_high = lax.axis_size("gx")
    size_low = lax.axis_size("gy")
    groups = size_high * size_low
    nbits = groups.bit_length() - 1
    block_rows = half_rows // groups
    device_index = lax.axis_index(("gx", "gy"))
    state = weights
    for level in range(LEVELS):
        bit_index = level % nbits
        side_bit = device_index >> bit_index & 1
        forward = level_matrix(interp_real[level], interp_imag[level])
        swapped = jnp.concatenate([forward[width:], forward[:width]], 0)
        matrix = jnp.where(side_bit == 0, forward, swapped)
        kept = lax.dynamic_slice_in_dim(state, side_bit * half_rows, half_rows, 0)
        sent = lax.dynamic_slice_in_dim(state, (1 - side_bit) * half_rows, half_rows, 0)
        received = from_partner(sent, ("gx", "gy"), bit_index)
        paired = jnp.concatenate([kept, received], 1)
        mixed = jnp.dot(paired, matrix, preferred_element_type=jnp.float32)
        mixed = jnp.swapaxes(mixed.reshape(half_rows, 2, width), 0, 1).reshape(pair_rows, width)
        state = rotate(mixed, travel * (level + 1.0)).astype(jnp.bfloat16)
    relaid = lax.all_to_all(
        state.reshape(2, groups, block_rows, width),
        ("gx", "gy"),
        split_axis=1,
        concat_axis=1,
        tiled=True,
    )
    relaid = relaid.reshape(pair_rows, width)
    evaluation = complex_block(eval_real, eval_imag)
    image = jnp.dot(relaid, evaluation, preferred_element_type=jnp.float32)
    return image.astype(jnp.bfloat16)


def solution(mesh):
    return jax.shard_map(
        local,
        mesh=mesh,
        in_specs=(P(("gx", "gy"), None), P(("gx", "gy"), None), P(), P(), P(), P()),
        out_specs=P(("gx", "gy"), None),
        check_vma=False,
    )
```

profile of v0, /device:TPU:1, one launch (start us, length us, event | category | flops | bytes accessed | tf_op | source)
XLA Modules:
  0.0 577.1 jit_solution(10148252568800266140)
XLA Ops:
  0.0 3.9 constant_dynamic-slice_fusion.1
  3.9 1.4 collective-permute-start
  6.5 15.8 %fusion.590 = (f32[16384,64]{0,1:T(8,128)S(1)}, f32[16384,64]{0,1:T(8,128)S(1)}) fusion(f32[16384,64]{0,1:T(8,128)} %param.7), kind=kLoop, calls=%fused_computation.741 | loop fusion | bytes 12582912 | tf_op jit(solution)/shard_map/cos | solution.py:35
  22.3 6.3 %fusion = f32[8192,256]{0,1:T(8,128)} fusion(bf16[8192,128]{1,0:T(8,128)(2,1)} %collective-permute-done, bf16[8192,128]{1,0:T(8,128)(2,1)S(1)} %get-tuple-element.35, bf16[64,64]{0,1:T(8,128)(2,1)S(1)} %get-tuple-element.153, bf16[64,64]{0,1:T(8,128)(2,1)S(1)} %get-tuple-element.144, bf16[64,64]{0,1:T(8,128)(2,1)S(1)} %get-tuple-element.140, ...), kind=kOutput, calls=%fused_computation.30 | convolution fusion | flops 1086390272 | bytes 12681217 | tf_op jit(solution)/shard_map/dot_general | solution.py:63
  28.6 3.9 copy.34
  33.6 1.7 fusion.45
  36.6 46.3 %collective-permute-done.1 = bf16[8192,128]{0,1:T(8,128)(2,1)} collective-permute-done((bf16[8192,128]{0,1:T(8,128)(2,1)}, bf16[8192,128]{0,1:T(8,128)(2,1)}, u32[]{:S(2)}, u32[]{:S(2)}) %collective-permute-start.1) | collective-permute-done | bytes 2097184 | tf_op jit(solution)/shard_map/ppermute | solution.py:10
  82.9 2.9 fusion.4
  86.7 1.3 copy-done
  88.0 15.9 %add_convert_fusion.6 = (bf16[16384,64]{0,1:T(8,128)(2,1)S(1)}, bf16[16384,64]{0,1:T(8,128)(2,1)S(1)}) fusion(f32[16384,128]{0,1:T(8,128)S(1)} %bitcast.409, f32[16384,64]{0,1:T(8,128)S(1)} %copy-done), kind=kLoop, calls=%fused_computation.74 | loop fusion | flops 9437184 | bytes 16777216 | tf_op jit(solution)/shard_map/convert.15
  103.9 1.6 fusion.43
  105.5 1.4 collective-permute-start.2
  106.9 45.3 %collective-permute-done.2 = bf16[8192,128]{0,1:T(8,128)(2,1)} collective-permute-done((bf16[8192,128]{0,1:T(8,128)(2,1)}, bf16[8192,128]{0,1:T(8,128)(2,1)}, u32[]{:S(2)}, u32[]{:S(2)}) %collective-permute-start.2) | collective-permute-done | bytes 2097184 | tf_op jit(solution)/shard_map/ppermute | solution.py:10
  152.2 2.9 fusion.8
  156.1 1.3 copy-done.1
  157.4 15.9 %add_convert_fusion.5 = (bf16[16384,64]{0,1:T(8,128)(2,1)S(1)}, bf16[16384,64]{0,1:T(8,128)(2,1)S(1)}) fusion(f32[16384,128]{0,1:T(8,128)S(1)} %bitcast.410, f32[16384,64]{0,1:T(8,128)S(1)} %copy-done.1), kind=kLoop, calls=%fused_computation.72 | loop fusion | flops 9437184 | bytes 16777216 | tf_op jit(solution)/shard_map/convert.13
  173.3 1.6 fusion.41
  174.9 3.1 collective-permute-start.3
  178.0 44.3 %collective-permute-done.3 = bf16[8192,128]{0,1:T(8,128)(2,1)} collective-permute-done((bf16[8192,128]{0,1:T(8,128)(2,1)}, bf16[8192,128]{0,1:T(8,128)(2,1)}, u32[]{:S(2)}, u32[]{:S(2)}) %collective-permute-start.3) | collective-permute-done | bytes 2097184 | tf_op jit(solution)/shard_map/ppermute | solution.py:10
  222.3 2.9 fusion.12
  227.4 15.9 %add_convert_fusion.4 = (bf16[16384,64]{0,1:T(8,128)(2,1)S(1)}, bf16[16384,64]{0,1:T(8,128)(2,1)S(1)}) fusion(f32[16384,128]{0,1:T(8,128)S(1)} %bitcast.411, f32[16384,64]{0,1:T(8,128)S(1)} %copy-done.2), kind=kLoop, calls=%fused_computation.70 | loop fusion | flops 9437184 | bytes 16777216 | tf_op jit(solution)/shard_map/convert.11
  243.4 1.6 fusion.39
  245.0 1.7 collective-permute-start.4
  246.6 43.6 %collective-permute-done.4 = bf16[8192,128]{0,1:T(8,128)(2,1)} collective-permute-done((bf16[8192,128]{0,1:T(8,128)(2,1)}, bf16[8192,128]{0,1:T(8,128)(2,1)}, u32[]{:S(2)}, u32[]{:S(2)}) %collective-permute-start.4) | collective-permute-done | bytes 2097184 | tf_op jit(solution)/shard_map/ppermute | solution.py:10
  290.2 2.9 fusion.16
  295.3 15.9 %add_convert_fusion.3 = (bf16[16384,64]{0,1:T(8,128)(2,1)S(1)}, bf16[16384,64]{0,1:T(8,128)(2,1)S(1)}) fusion(f32[16384,128]{0,1:T(8,128)S(1)} %bitcast.412, f32[16384,64]{0,1:T(8,128)S(1)} %copy-done.3), kind=kLoop, calls=%fused_computation.68 | loop fusion | flops 9437184 | bytes 16777216 | tf_op jit(solution)/shard_map/convert.9
  311.3 1.6 fusion.37
  312.9 3.2 collective-permute-start.5
  316.0 42.7 %collective-permute-done.5 = bf16[8192,128]{0,1:T(8,128)(2,1)} collective-permute-done((bf16[8192,128]{0,1:T(8,128)(2,1)}, bf16[8192,128]{0,1:T(8,128)(2,1)}, u32[]{:S(2)}, u32[]{:S(2)}) %collective-permute-start.5) | collective-permute-done | bytes 2097184 | tf_op jit(solution)/shard_map/ppermute | solution.py:10
  358.7 2.9 fusion.20
  363.9 15.9 %add_convert_fusion.2 = (bf16[16384,64]{0,1:T(8,128)(2,1)S(1)}, bf16[16384,64]{0,1:T(8,128)(2,1)S(1)}) fusion(f32[16384,128]{0,1:T(8,128)S(1)} %bitcast.413, f32[16384,64]{0,1:T(8,128)S(1)} %copy-done.4), kind=kLoop, calls=%fused_computation.66 | loop fusion | flops 9437184 | bytes 16777216 | tf_op jit(solution)/shard_map/convert.7
  379.8 1.6 fusion.35
  381.4 3.0 collective-permute-start.6
  384.4 42.0 %collective-permute-done.6 = bf16[8192,128]{0,1:T(8,128)(2,1)} collective-permute-done((bf16[8192,128]{0,1:T(8,128)(2,1)}, bf16[8192,128]{0,1:T(8,128)(2,1)}, u32[]{:S(2)}, u32[]{:S(2)}) %collective-permute-start.6) | collective-permute-done | bytes 2097184 | tf_op jit(solution)/shard_map/ppermute | solution.py:10
  426.3 2.9 fusion.24
  431.5 15.9 %add_convert_fusion.1 = (bf16[16384,64]{0,1:T(8,128)(2,1)S(1)}, bf16[16384,64]{0,1:T(8,128)(2,1)S(1)}) fusion(f32[16384,128]{0,1:T(8,128)S(1)} %bitcast.414, f32[16384,64]{0,1:T(8,128)S(1)} %copy-done.5), kind=kLoop, calls=%fused_computation.64 | loop fusion | flops 9437184 | bytes 16777216 | tf_op jit(solution)/shard_map/convert.5
  447.8 5.2 collective-permute-start.7
  453.0 3.8 collective-permute-done.7
  456.8 1.3 fusion.28
  459.0 16.8 %subtract_convert_fusion = (bf16[16384,64]{0,1:T(8,128)(2,1)}, bf16[16384,64]{0,1:T(8,128)(2,1)}) fusion(f32[16384,128]{0,1:T(8,128)S(1)} %bitcast.415, f32[16384,64]{0,1:T(8,128)S(1)} %copy-done.5), kind=kLoop, calls=%fused_computation.63 | loop fusion | flops 9437184 | bytes 16777216 | tf_op jit(solution)/shard_map/convert.3
  475.9 6.7 %concatenate.597 = bf16[2,128,64,64]{2,1,0,3:T(8,128)(2,1)} reshape(bf16[16384,64]{0,1:T(8,128)(2,1)} %get-tuple-element.7) | data formatting | bytes 4194304 | tf_op jit(solution)/shard_map/concatenate | solution.py:37
  482.6 5.5 concatenate.598
  488.1 8.4 %pad_maximum_fusion = bf16[2,128,64,128]{2,1,0,3:T(8,128)(2,1)} fusion(bf16[2,128,64,64]{2,1,0,3:T(8,128)(2,1)} %concatenate.598, bf16[2,128,64,64]{2,1,0,3:T(8,128)(2,1)} %concatenate.597), kind=kLoop, calls=%fused_computation.1 | loop fusion | flops 2097152 | bytes 8388608 | tf_op jit(solution)/shard_map/concatenate | solution.py:37
  496.5 11.4 %copy.32 = bf16[2,128,64,128]{3,2,0,1:T(8,128)(2,1)} copy(bf16[2,128,64,128]{2,1,0,3:T(8,128)(2,1)} %pad_maximum_fusion) | data formatting | bytes 8388608 | tf_op jit(solution)/shard_map/concatenate | solution.py:37
  507.9 9.9 %all-to-all-start = ((bf16[2,128,64,128]{3,2,0,1:T(8,128)(2,1)}), bf16[2,128,64,128]{3,2,0,1:T(8,128)(2,1)}, u32[]{:S(2)}, u32[]{:S(2)}) async-start(bf16[2,128,64,128]{3,2,0,1:T(8,128)(2,1)} %copy.32), calls=%async_computation | async-start | bytes 8388608 | tf_op jit(solution)/shard_map/all_to_all | solution.py:66
  517.8 52.4 %all-to-all-done = bf16[2,128,64,128]{3,2,0,1:T(8,128)(2,1)} async-done(((bf16[2,128,64,128]{3,2,0,1:T(8,128)(2,1)}), bf16[2,128,64,128]{3,2,0,1:T(8,128)(2,1)}, u32[]{:S(2)}, u32[]{:S(2)}) %all-to-all-start) | async-done | bytes 4194336 | tf_op jit(solution)/shard_map/all_to_all | solution.py:66
  570.2 3.1 copy.33
  573.3 3.3 convolution_convert_fusion
  (48 shorter events, 15.5 us)
Async XLA Ops:
  0.0 5.3 copy-start.7
  3.9 18.5 %collective-permute-start = (bf16[8192,128]{1,0:T(8,128)(2,1)}, bf16[8192,128]{1,0:T(8,128)(2,1)}, u32[]{:S(2)}, u32[]{:S(2)}) collective-permute-start(bf16[8192,128]{1,0:T(8,128)(2,1)} %get-tuple-element.36), channel_id=1, source_target_pairs={{0,1},{1,0},{2,3},{3,2},{4,5},{5,4},{6,7},{7,6},{8,9},{9,8},{10,11... | collective-permute-start | bytes 6291464 | tf_op jit(solution)/shard_map/ppermute | solution.py:10
  35.3 47.6 %collective-permute-start.1 = (bf16[8192,128]{0,1:T(8,128)(2,1)}, bf16[8192,128]{0,1:T(8,128)(2,1)}, u32[]{:S(2)}, u32[]{:S(2)}) collective-permute-start(bf16[8192,128]{0,1:T(8,128)(2,1)} %get-tuple-element.34), channel_id=1, source_target_pairs={{0,2},{1,3},{2,0},{3,1},{4,6},{5,7},{6,4},{7,5},{8,10},{9,11},{10,... | collective-permute-start | bytes 6291464 | tf_op jit(solution)/shard_map/ppermute | solution.py:10
  85.8 2.2 copy-start
  105.5 46.7 %collective-permute-start.2 = (bf16[8192,128]{0,1:T(8,128)(2,1)}, bf16[8192,128]{0,1:T(8,128)(2,1)}, u32[]{:S(2)}, u32[]{:S(2)}) collective-permute-start(bf16[8192,128]{0,1:T(8,128)(2,1)} %get-tuple-element.32), channel_id=1, source_target_pairs={{0,4},{1,5},{2,6},{3,7},{4,0},{5,1},{6,2},{7,3},{8,12},{9,13},{10,... | collective-permute-start | bytes 6291464 | tf_op jit(solution)/shard_map/ppermute | solution.py:10
  155.2 2.2 copy-start.1
  174.9 47.4 %collective-permute-start.3 = (bf16[8192,128]{0,1:T(8,128)(2,1)}, bf16[8192,128]{0,1:T(8,128)(2,1)}, u32[]{:S(2)}, u32[]{:S(2)}) collective-permute-start(bf16[8192,128]{0,1:T(8,128)(2,1)} %get-tuple-element.30), channel_id=1, source_target_pairs={{0,8},{1,9},{2,10},{3,11},{4,12},{5,13},{6,14},{7,15},{8,0},{9,1},... | collective-permute-start | bytes 6291464 | tf_op jit(solution)/shard_map/ppermute | solution.py:10
  225.2 2.2 copy-start.2
  245.0 45.3 %collective-permute-start.4 = (bf16[8192,128]{0,1:T(8,128)(2,1)}, bf16[8192,128]{0,1:T(8,128)(2,1)}, u32[]{:S(2)}, u32[]{:S(2)}) collective-permute-start(bf16[8192,128]{0,1:T(8,128)(2,1)} %get-tuple-element.28), channel_id=1, source_target_pairs={{0,16},{1,17},{2,18},{3,19},{4,20},{5,21},{6,22},{7,23},{8,24},{9,... | collective-permute-start | bytes 6291464 | tf_op jit(solution)/shard_map/ppermute | solution.py:10
  293.1 2.2 copy-start.3
  312.9 45.9 %collective-permute-start.5 = (bf16[8192,128]{0,1:T(8,128)(2,1)}, bf16[8192,128]{0,1:T(8,128)(2,1)}, u32[]{:S(2)}, u32[]{:S(2)}) collective-permute-start(bf16[8192,128]{0,1:T(8,128)(2,1)} %get-tuple-element.26), channel_id=1, source_target_pairs={{0,32},{1,33},{2,34},{3,35},{4,36},{5,37},{6,38},{7,39},{8,40},{9,... | collective-permute-start | bytes 6291464 | tf_op jit(solution)/shard_map/ppermute | solution.py:10
  361.7 2.2 copy-start.4
  381.4 45.0 %collective-permute-start.6 = (bf16[8192,128]{0,1:T(8,128)(2,1)}, bf16[8192,128]{0,1:T(8,128)(2,1)}, u32[]{:S(2)}, u32[]{:S(2)}) collective-permute-start(bf16[8192,128]{0,1:T(8,128)(2,1)} %get-tuple-element.24), channel_id=1, source_target_pairs={{0,64},{1,65},{2,66},{3,67},{4,68},{5,69},{6,70},{7,71},{8,72},{9,... | collective-permute-start | bytes 6291464 | tf_op jit(solution)/shard_map/ppermute | solution.py:10
  429.3 2.2 copy-start.5
  447.8 9.0 %collective-permute-start.7 = (bf16[8192,128]{0,1:T(8,128)(2,1)S(1)}, bf16[8192,128]{0,1:T(8,128)(2,1)S(1)}, u32[]{:S(2)}, u32[]{:S(2)}) collective-permute-start(bf16[8192,128]{0,1:T(8,128)(2,1)S(1)} %get-tuple-element.22), channel_id=1, source_target_pairs={{0,1},{1,0},{2,3},{3,2},{4,5},{5,4},{6,7},{7,6},{8,9},{9,8},{10,11... | collective-permute-start | bytes 6291464 | tf_op jit(solution)/shard_map/ppermute | solution.py:10
  475.9 6.7 %copy-start.6 = (bf16[16384,64]{0,1:T(8,128)(2,1)S(1)}, bf16[16384,64]{0,1:T(8,128)(2,1)}, u32[]{:S(2)}) copy-start(bf16[16384,64]{0,1:T(8,128)(2,1)} %get-tuple-element.8) | copy-start | bytes 6291460
  507.9 9.9 %copy-start.8 = (bf16[64,64]{1,0:T(8,128)(2,1)S(1)}, bf16[64,64]{1,0:T(8,128)(2,1)}, u32[]{:S(2)}) copy-start(bf16[64,64]{1,0:T(8,128)(2,1)} %param.11) | copy-start | bytes 24580
  507.9 62.3 %all-to-all-start = ((bf16[2,128,64,128]{3,2,0,1:T(8,128)(2,1)}), bf16[2,128,64,128]{3,2,0,1:T(8,128)(2,1)}, u32[]{:S(2)}, u32[]{:S(2)}) async-start(bf16[2,128,64,128]{3,2,0,1:T(8,128)(2,1)} %copy.32), calls=%async_computation | async-start | bytes 8388608 | tf_op jit(solution)/shard_map/all_to_all | solution.py:66
  517.8 55.5 %copy-start.9 = (bf16[64,64]{1,0:T(8,128)(2,1)S(1)}, bf16[64,64]{1,0:T(8,128)(2,1)}, u32[]{:S(2)}) copy-start(bf16[64,64]{1,0:T(8,128)(2,1)} %param.10) | copy-start | bytes 24580
where the time goes:
time: 586 us; the launch traced here: 577 us
  waiting for transfers between devices  320 us (55%)
  other arithmetic  132 us (23%)
  local copies, waits for them, and re-layouts  65.6 us (11%)
  starting transfers between devices  30 us (5%)
  matrix products  28.6 us (5%)
    ppermute x8, waiting for transfers between devices, from_partner(): lax.ppermute(x, axis, [(i, i ^ 1 << stride) for i in range(lax.axis_size(...  268 us
    another operation x8, other arithmetic  113 us
    all_to_all x1, waiting for transfers between devices, local(): lax.all_to_all(state.reshape(2, groups, block_rows, width), ('gx', 'gy'),...  52.4 us
    dot_general x8, matrix products, local(): mixed = jnp.dot(paired, matrix, preferred_element_type=jnp.float32)  25.2 us
    concatenate x3, local copies, waits for them, and re-layouts, rotate(): jnp.concatenate([real_part * cosine - imag_part * sine, real_part * sine...  23.6 us
    ppermute x8, starting transfers between devices, from_partner(): lax.ppermute(x, axis, [(i, i ^ 1 << stride) for i in range(lax.axis_size(...  20.1 us
    concatenate x8, other arithmetic, rotate(): jnp.concatenate([real_part * cosine - imag_part * sine, real_part * sine...  18.5 us
    cos x1, local copies, waits for them, and re-layouts, rotate(): cosine = jnp.cos(angle)  15.8 us
  transfers between devices with their start and end apart: 9, of which 8 were waited for; matrix products, arithmetic and copies ran while one was open for 3% of the time, Pallas kernels for 0%

commit v1 on v0

v1 whole, which is shorter than its diff:
```python
import functools

import jax
import jax.numpy as jnp
from jax import lax
from jax.experimental import pallas as pl
from jax.experimental.pallas import tpu as pltpu
from jax.sharding import PartitionSpec as P

LEVELS = 8
GROUPS = 128
HALVES = GROUPS // 2
ROWS = 16
LANES = 128
SCALE = 40.0


def odd_bits(n):
    return bin(n).count("1") % 2


def level_matrices(real, imag):
    def block(kind_in, child_in, kind_out, child_out):
        if kind_in == kind_out:
            return real[child_out, child_in].T
        part = imag[child_out, child_in].T
        return -part if kind_in == 1 else part

    def build(rows, columns):
        return jnp.concatenate(
            [jnp.concatenate([block(*r, *c) for c in columns], 1) for r in rows], 0
        )

    return block, build


KIND_CHILD = [(k, c) for k in range(2) for c in range(2)]
KIND_CHILD_SWAPPED = [(k, 1 - c) for k in range(2) for c in range(2)]
CHILD_KIND = [(k, c) for c in range(2) for k in range(2)]


def all_matrices(interp_real, interp_imag, eval_real, eval_imag):
    mats = []
    for level in range(LEVELS):
        _, build = level_matrices(interp_real[level], interp_imag[level])
        rows_even = CHILD_KIND if level == 0 else KIND_CHILD
        rows_odd = CHILD_KIND if level == 0 else KIND_CHILD_SWAPPED
        mats.append(build(rows_even, KIND_CHILD))
        mats.append(build(rows_odd, KIND_CHILD_SWAPPED))
    zero = jnp.zeros_like(eval_real)
    real = jnp.stack([jnp.stack([eval_real, zero]), jnp.stack([zero, eval_real])])
    imag = jnp.stack([jnp.stack([eval_imag, zero]), jnp.stack([zero, eval_imag])])
    _, build = level_matrices(real, imag)
    mats.append(build(KIND_CHILD, CHILD_KIND))
    mats.append(build(KIND_CHILD_SWAPPED, CHILD_KIND))
    return jnp.stack(mats)


def sine_cosine(angle):
    half = angle * 0.5
    sq = half * half
    sine = half * (1.0 + sq * (-1.6666667e-1 + sq * (8.3333310e-3 + sq * (-1.9840874e-4 + sq * (2.7525562e-6 - 2.3889859e-8 * sq)))))
    cosine = 1.0 + sq * (-0.5 + sq * (4.1666642e-2 + sq * (-1.3888378e-3 + sq * (2.4760495e-5 - 2.6051615e-7 * sq))))
    return 2.0 * sine * cosine, 1.0 - 2.0 * sine * sine


def wave(weights, codes, mats, out, re, im, cos1, sin1, cosl, sinl):
    low = lax.broadcasted_iota(jnp.int32, (ROWS, LANES), 1) < LANES // 2
    flat = lambda tiles: jnp.concatenate(tiles, 0)

    def owner(parity, v):
        return 2 * v + (odd_bits(v) + parity) % 2

    def start(blk, _):
        for parity in range(2):
            for i in range(8):
                v = blk * 8 + i
                odd = (odd_bits(i) + parity) % 2
                flip = lax.rem(blk + blk // 2 + blk // 4, 2)
                d = 2 * v + odd + flip * (1 - 2 * odd)
                angle = jnp.log2(codes(d).astype(jnp.float32)) * (1.0 / SCALE)
                sine, cosine = sine_cosine(angle)
                for ref in (cos1, cosl):
                    ref[parity, v] = cosine
                for ref in (sin1, sinl):
                    ref[parity, v] = sine
        return 0

    lax.fori_loop(0, HALVES // 8, start, 0)

    def rotate_store(mixed, parity, vs, level):
        for k, v in enumerate(vs):
            real = mixed[k * ROWS:(k + 1) * ROWS, :LANES]
            imag = mixed[k * ROWS:(k + 1) * ROWS, LANES:]
            cosine, sine = cosl[parity, v], sinl[parity, v]
            re[parity, v] = (real * cosine - imag * sine).astype(jnp.bfloat16)
            im[parity, v] = (real * sine + imag * cosine).astype(jnp.bfloat16)
            if level < LEVELS - 1:
                c, s = cos1[parity, v], sin1[parity, v]
                cosl[parity, v] = cosine * c - sine * s
                sinl[parity, v] = cosine * s + sine * c

    blocks = 4
    span = HALVES // blocks

    def first(blk, _):
        flip = lax.rem(blk + blk // 2, 2)
        for parity in range(2):
            vs = [blk * span + i for i in range(span)]
            left, right = [], []
            for i, v in enumerate(vs):
                odd = (odd_bits(i) + parity) % 2
                s = odd + flip * (1 - 2 * odd)
                left.append(weights(s, 2 * v))
                right.append(weights(s, 2 * v + 1))
            x = jnp.concatenate([flat(left), flat(right)], 1)
            mixed = jnp.dot(x, mats[parity], preferred_element_type=jnp.float32)
            rotate_store(mixed, parity, vs, 0)
        return 0

    lax.fori_loop(0, blocks, first, 0)

    for level in range(1, LEVELS):
        bit = level % 7 - 1
        step = 0 if bit < 0 else 1 << bit
        if bit < 4:
            base = [i for i in range(span)]
            stride = span
        else:
            base = [i + 8 * 0 for i in range(8)] + [i + (1 << bit) for i in range(8)]
            stride = None

        def body(blk, _, level=level, bit=bit, step=step, base=base, stride=stride):
            if stride is not None:
                offset = blk * stride
            elif bit == 4:
                offset = lax.rem(blk, 2) * 8 + blk // 2 * 32
            else:
                offset = blk * 8
            sel = [[], []]
            vs = [offset + i for i in base]
            ws = [offset + (i ^ step) for i in base]
            pieces = [[[], []], [[], []]]
            if bit < 0:
                flip = lax.rem(blk + blk // 2, 2)
                masks = [low != (flip == 1), low == (flip == 1)]
            for i, v, w in zip(base, vs, ws):
                if bit < 0:
                    mask = masks[odd_bits(i)]
                else:
                    mask = low if (i >> bit) % 2 == 0 else jnp.logical_not(low)
                for kind, ref in enumerate((re, im)):
                    even, odd = ref[0, v], ref[1, w]
                    pieces[0][kind].append(jnp.where(mask, even, odd))
                    pieces[1][kind].append(jnp.where(mask, odd, even))
            mixed = []
            for parity in range(2):
                x = jnp.concatenate([flat(pieces[parity][0]), flat(pieces[parity][1])], 1)
                mixed.append(jnp.dot(x, mats[2 * level + parity], preferred_element_type=jnp.float32))
            for parity in range(2):
                rotate_store(mixed[parity], parity, (vs, ws)[parity], level)
            return 0

        lax.fori_loop(0, blocks, body, 0)

    def last(blk, _):
        flip = lax.rem(blk + blk // 2, 2)
        for parity in range(2):
            vs = [blk * span + i for i in range(span)]
            x = jnp.concatenate([flat([re[parity, v] for v in vs]), flat([im[parity, v] for v in vs])], 1)
            image = jnp.dot(x, mats[2 * LEVELS + parity], preferred_element_type=jnp.float32).astype(jnp.bfloat16)
            for i, v in enumerate(vs):
                odd = (odd_bits(i) + parity) % 2
                d = 2 * v + odd + flip * (1 - 2 * odd)
                for s in range(2):
                    out[s, d] = image[i * ROWS:(i + 1) * ROWS, s * LANES:(s + 1) * LANES]
        return 0

    lax.fori_loop(0, blocks, last, 0)


def compute_kernel(arrived, mats, out, *scratch):
    wave(lambda s, d: arrived[s, d], lambda d: arrived[2, d], mats, out, *scratch)


def wave_scratch():
    state = pltpu.VMEM((2, HALVES, ROWS, LANES), jnp.bfloat16)
    phase = pltpu.VMEM((2, HALVES, ROWS, LANES), jnp.float32)
    return [state, state, phase, phase, phase, phase]


def local(weights, travel, interp_real, interp_imag, eval_real, eval_imag):
    pair_rows, width = weights.shape
    block_rows = pair_rows // (2 * GROUPS)
    me = lax.axis_index(("gx", "gy"))
    odd = lax.rem(lax.population_count(me), 2)
    phases = travel.reshape(2, GROUPS, block_rows, width // 2)
    phases = jnp.where(odd == 1, phases[::-1], phases)
    codes = jnp.exp2(SCALE * jnp.concatenate([phases[0], phases[1]], -1)).astype(jnp.bfloat16)
    sent = jnp.concatenate([weights.reshape(2, GROUPS, block_rows, width), codes[None]], 0)
    arrived = lax.all_to_all(sent, ("gx", "gy"), split_axis=1, concat_axis=1, tiled=True)
    mats = all_matrices(interp_real, interp_imag, eval_real, eval_imag)
    image = pl.pallas_call(
        compute_kernel,
        grid=(block_rows // ROWS,),
        in_specs=[
            pl.BlockSpec((3, GROUPS, ROWS, LANES), lambda w: (0, 0, w, 0)),
            pl.BlockSpec(mats.shape, lambda w: (0, 0, 0)),
        ],
        out_specs=pl.BlockSpec((2, GROUPS, ROWS, LANES), lambda w: (0, 0, w, 0)),
        out_shape=jax.ShapeDtypeStruct((2, GROUPS, block_rows, width), jnp.bfloat16),
        scratch_shapes=wave_scratch(),
        compiler_params=pltpu.CompilerParams(vmem_limit_bytes=40 << 20),
    )(arrived, mats)
    return image.reshape(pair_rows, width)


def solution(mesh):
    return jax.shard_map(
        local,
        mesh=mesh,
        in_specs=(P(("gx", "gy"), None), P(("gx", "gy"), None), P(), P(), P(), P()),
        out_specs=P(("gx", "gy"), None),
        check_vma=False,
    )
```

time: 586 us -> 161 us (0.27); the launches traced: 577 us -> 159 us
  waiting for transfers between devices: 320 us -> 73.7 us
  other arithmetic: 132 us -> 11.9 us
  local copies, waits for them, and re-layouts: 65.6 us -> 20.1 us
  Pallas kernels: 0 us -> 41.3 us
  matrix products: 28.6 us -> 0 us
  starting transfers between devices: 30 us -> 11.9 us
    ppermute x8 -> x0, waiting for transfers between devices: 268 us -> none  [from_partner(): lax.ppermute(x, axis, [(i, i ^ 1 << stride) for i in range(lax.axis_size(...]
    another operation x8 -> x1, other arithmetic: 113 us -> 0.13 us  [all_matrices(): return jnp.stack(mats)]
    pallas_call x0 -> x1, Pallas kernels: none -> 41.3 us  [local(): pl.pallas_call(compute_kernel, grid=(block_rows // ROWS,), in_specs=[pl.B...]
    dot_general x9 -> x0, matrix products: 28.6 us -> none  [the longest x8 25.2 us: local(): mixed = jnp.dot(paired, matrix, preferred_element_type=jnp.float32)]
    all_to_all x1, waiting for transfers between devices: 52.4 us -> 73.7 us  [local(): lax.all_to_all(sent, ('gx', 'gy'), split_axis=1, concat_axis=1, tiled=True)]
    ppermute x8 -> x0, starting transfers between devices: 20.1 us -> none  [from_partner(): lax.ppermute(x, axis, [(i, i ^ 1 << stride) for i in range(lax.axis_size(...]
    concatenate x3 -> x1, local copies, waits for them, and re-layouts: 23.6 us -> 4.12 us  [local(): jnp.concatenate([weights.reshape(2, GROUPS, block_rows, width), codes[Non...]
    concatenate x8 -> x1, other arithmetic: 18.5 us -> 0.54 us  [local(): jnp.concatenate([weights.reshape(2, GROUPS, block_rows, width), codes[Non...]
  transfers between devices with their start and end apart: 9 -> 1, of which waited for: 8 -> 1; matrix products, arithmetic and copies ran while one was open for 3% -> 3% of each run, Pallas kernels for 0% -> 0%
where the time goes in v1:
time: 161 us; the launch traced here: 159 us
  waiting for transfers between devices  73.7 us (46%)
  Pallas kernels  41.3 us (26%)
  local copies, waits for them, and re-layouts  20.1 us (12%)
  other arithmetic  11.9 us (7%)
  starting transfers between devices  11.9 us (7%)
    all_to_all x1, waiting for transfers between devices, local(): lax.all_to_all(sent, ('gx', 'gy'), split_axis=1, concat_axis=1, tiled=True)  73.7 us
    pallas_call x1, Pallas kernels, local(): pl.pallas_call(compute_kernel, grid=(block_rows // ROWS,), in_specs=[pl.B...  41.3 us
    all_to_all x1, starting transfers between devices, local(): lax.all_to_all(sent, ('gx', 'gy'), split_axis=1, concat_axis=1, tiled=True)  11.9 us
    select_n x1, other arithmetic, local(): phases = jnp.where(odd == 1, phases[::-1], phases)  7.78 us
    reshape x1, local copies, waits for them, and re-layouts, local(): phases = travel.reshape(2, GROUPS, block_rows, width // 2)  6.95 us
    all_to_all x1, local copies, waits for them, and re-layouts, local(): lax.all_to_all(sent, ('gx', 'gy'), split_axis=1, concat_axis=1, tiled=True)  4.28 us
    concatenate x1, local copies, waits for them, and re-layouts, local(): jnp.concatenate([weights.reshape(2, GROUPS, block_rows, width), codes[Non...  4.12 us
  transfers between devices with their start and end apart: 1, of which 1 were waited for; matrix products, arithmetic and copies ran while one was open for 3% of the time, Pallas kernels for 0%

profile of v1, /device:TPU:1, one launch (start us, length us, event | category | flops | bytes accessed | tf_op | source)
XLA Modules:
  0.0 159.4 jit_solution(14697656841982630966)
XLA Ops:
  0.0 6.9 %copy.67 = f32[16384,64]{1,0:T(8,128)} copy(f32[16384,64]{0,1:T(8,128)} %param.7) | data formatting | bytes 8388608 | tf_op jit(solution)/shard_map/reshape | solution.py:197
  6.9 7.8 %reverse_select_fusion = f32[2,128,64,64]{3,2,1,0:T(8,128)S(1)} fusion(f32[2,128,64,64]{3,2,1,0:T(8,128)} %bitcast.461, pred[]{:T(512)S(6)} %eq.3), kind=kLoop, calls=%fused_computation | loop fusion | flops 1048576 | bytes 8388609 | tf_op jit(solution)/shard_map/jit(_where)/select_n | solution.py:198
  14.7 1.7 %fusion.56 = (f32[1,128,64,64]{3,2,1,0:T(8,128)S(1)}, f32[1,128,64,64]{3,2,1,0:T(8,128)S(1)}) fusion(f32[2,128,64,64]{3,2,1,0:T(8,128)S(1)} %reverse_select_fusion), kind=kLoop, calls=%fused_computation.153 | loop fusion | bytes 8388608 | tf_op jit(solution)/shard_map/slice | solution.py:199
  16.4 1.2 fusion.1
  17.6 1.0 copy-done
  18.6 0.5 pad_maximum_fusion
  19.1 4.1 %copy.47 = bf16[3,128,64,128]{3,2,0,1:T(8,128)(2,1)} copy(bf16[3,128,64,128]{3,2,1,0:T(8,128)(2,1)S(1)} %pad_maximum_fusion) | data formatting | bytes 12582912 | tf_op jit(solution)/shard_map/concatenate | solution.py:200
  23.3 11.9 %all-to-all-start = ((bf16[3,128,64,128]{3,2,0,1:T(8,128)(2,1)}), bf16[3,128,64,128]{3,2,0,1:T(8,128)(2,1)}, u32[]{:S(2)}, u32[]{:S(2)}) async-start(bf16[3,128,64,128]{3,2,0,1:T(8,128)(2,1)} %copy.47), calls=%async_computation | async-start | bytes 12582912 | tf_op jit(solution)/shard_map/all_to_all | solution.py:201
  35.2 0.0 copy-start.4
  35.3 0.1 copy.69
  35.4 0.1 copy.68
  35.6 0.1 copy.71
  35.7 0.1 copy.70
  35.8 0.1 copy.73
  35.9 0.1 copy.72
  36.0 0.1 copy.75
  36.1 0.1 copy.74
  36.2 0.1 copy.77
  36.3 0.1 copy.76
  36.4 0.1 copy.79
  36.5 0.1 copy.78
  36.6 0.1 copy.81
  36.8 0.1 copy.80
  36.9 0.1 copy.83
  37.0 0.1 copy.82
  37.1 0.1 copy.64
  37.2 0.1 copy.65
  37.4 0.1 fusion.2
  37.5 0.1 fusion.3
  37.7 0.1 fusion.4
  37.8 0.1 fusion.5
  38.0 0.1 fusion.6
  38.1 0.1 fusion.7
  38.3 0.1 fusion.8
  38.4 0.1 fusion.9
  38.6 0.1 fusion.10
  38.7 0.1 fusion.11
  38.9 0.1 fusion.12
  39.1 0.1 fusion.13
  39.2 0.1 fusion.14
  39.4 0.1 fusion.15
  39.5 0.1 fusion.16
  39.7 0.1 fusion.17
  39.9 0.1 fusion.18
  40.0 0.1 fusion.19.mats
  40.1 73.7 %all-to-all-done = bf16[3,128,64,128]{3,2,0,1:T(8,128)(2,1)} async-done(((bf16[3,128,64,128]{3,2,0,1:T(8,128)(2,1)}), bf16[3,128,64,128]{3,2,0,1:T(8,128)(2,1)}, u32[]{:S(2)}, u32[]{:S(2)}) %all-to-all-start) | async-done | bytes 6291488 | tf_op jit(solution)/shard_map/all_to_all | solution.py:201
  113.8 4.3 %copy.66.arrived = bf16[3,128,64,128]{3,2,1,0:T(8,128)(2,1)S(1)} copy(bf16[3,128,64,128]{3,2,0,1:T(8,128)(2,1)} %all-to-all-done) | data formatting | bytes 12582912 | tf_op jit(solution)/shard_map/all_to_all | solution.py:201
  118.1 41.3 %shard_map.64 = bf16[2,128,64,128]{3,2,1,0:T(8,128)(2,1)} custom-call(bf16[3,128,64,128]{3,2,1,0:T(8,128)(2,1)S(1)} %copy.66.arrived, bf16[18,256,256]{2,1,0:T(8,128)(2,1)S(1)} %fusion.19.mats), custom_call_target="tpu_custom_call" | custom-call | tf_op jit(solution)/shard_map/pallas_call | solution.py:203
  (31 shorter events, 0.4 us)
Async XLA Ops:
  16.4 2.2 %copy-start = (bf16[16384,128]{1,0:T(8,128)(2,1)S(1)}, bf16[16384,128]{1,0:T(8,128)(2,1)}, u32[]{:S(2)}) copy-start(bf16[16384,128]{1,0:T(8,128)(2,1)} %param.6) | copy-start | bytes 12582916
  23.3 11.9 %copy-start.1 = (bf16[8,2,2,64,64]{4,3,2,1,0:T(8,128)(2,1)S(1)}, bf16[8,2,2,64,64]{4,3,2,1,0:T(8,128)(2,1)}, u32[]{:S(2)}) copy-start(bf16[8,2,2,64,64]{4,3,2,1,0:T(8,128)(2,1)} %param.9) | copy-start | bytes 786436
  23.3 12.1 %copy-start.2 = (bf16[8,2,2,64,64]{4,3,2,1,0:T(8,128)(2,1)S(1)}, bf16[8,2,2,64,64]{4,3,2,1,0:T(8,128)(2,1)}, u32[]{:S(2)}) copy-start(bf16[8,2,2,64,64]{4,3,2,1,0:T(8,128)(2,1)} %param.8) | copy-start | bytes 786436
  23.3 90.5 %all-to-all-start = ((bf16[3,128,64,128]{3,2,0,1:T(8,128)(2,1)}), bf16[3,128,64,128]{3,2,0,1:T(8,128)(2,1)}, u32[]{:S(2)}, u32[]{:S(2)}) async-start(bf16[3,128,64,128]{3,2,0,1:T(8,128)(2,1)} %copy.47), calls=%async_computation | async-start | bytes 12582912 | tf_op jit(solution)/shard_map/all_to_all | solution.py:201
  35.2 1.9 %copy-start.3 = (bf16[64,64]{1,0:T(8,128)(2,1)S(1)}, bf16[64,64]{1,0:T(8,128)(2,1)}, u32[]{:S(2)}) copy-start(bf16[64,64]{1,0:T(8,128)(2,1)} %param.10) | copy-start | bytes 24580
  35.2 2.0 %copy-start.4 = (bf16[64,64]{1,0:T(8,128)(2,1)S(1)}, bf16[64,64]{1,0:T(8,128)(2,1)}, u32[]{:S(2)}) copy-start(bf16[64,64]{1,0:T(8,128)(2,1)} %param.11) | copy-start | bytes 24580

commit v2 on v0

v2 whole, which is shorter than its diff:
```python
import jax
import jax.numpy as jnp
from jax import lax
from jax.experimental import pallas as pl
from jax.experimental.pallas import tpu as pltpu
from jax.sharding import PartitionSpec as P

MESH = pl.DeviceIdType.MESH
LEVELS = 8
GROUPS = 128
HALVES = GROUPS // 2
ROWS = 16
WAVES = 4
LANES = 128
HALF = LANES // 2
SPAN = 16
SCALE = 40.0
DIGITS = (2, 4, 4, 4)
CODES = 2
ORDERS = (("xyz", "yzx", "zxy"), ("zxy", "xyz", "yzx"), ("xyz", "yzx", "zxy"), ("xyz", "yzx", "zxy"))


def odd_bits(n):
    return bin(n).count("1") % 2


def digits(d):
    return d // 64, d // 16 % 4, d // 4 % 4, d % 4


def owner(parity, v):
    return 2 * v + (odd_bits(v) + parity) % 2


def sine_cosine(angle):
    half = angle * 0.5
    sq = half * half
    sine = half * (1.0 + sq * (-1.6666667e-1 + sq * (8.3333310e-3 + sq * (-1.9840874e-4 + sq * (2.7525562e-6 - 2.3889859e-8 * sq)))))
    cosine = 1.0 + sq * (-0.5 + sq * (4.1666642e-2 + sq * (-1.3888378e-3 + sq * (2.4760495e-5 - 2.6051615e-7 * sq))))
    twice = 2.0 * sine
    return twice * cosine, 1.0 - twice * sine


def build_matrices(real, imag, eval_real, eval_imag, mats):
    flip = lambda parity, child: (child + parity) % 2

    def halves(level):
        tr = [[real[level, c, e].astype(jnp.float32).T for e in range(2)] for c in range(2)]
        ti = [[imag[level, c, e].astype(jnp.float32).T for e in range(2)] for c in range(2)]

        def rows(kind, e, parity):
            a, b = flip(parity, 0), flip(parity, 1)
            if kind == 0:
                parts = [tr[a][e], tr[b][e], ti[a][e], ti[b][e]]
            else:
                parts = [-ti[a][e], -ti[b][e], tr[a][e], tr[b][e]]
            return jnp.concatenate(parts, 1).astype(jnp.bfloat16)

        return rows

    rows = halves(0)
    for parity in range(2):
        for e in range(2):
            for kind in range(2):
                mats[parity, (2 * e + kind) * HALF:(2 * e + kind + 1) * HALF] = rows(kind, e, parity)

    def level_body(level, _):
        rows = halves(level)
        for parity in range(2):
            for kind in range(2):
                for e in range(2):
                    at = 2 * kind + flip(parity, e)
                    mats[2 * level + parity, at * HALF:(at + 1) * HALF] = rows(kind, e, parity)
        return 0

    lax.fori_loop(1, LEVELS, level_body, 0)
    er = eval_real[...].astype(jnp.float32).T
    ei = eval_imag[...].astype(jnp.float32).T
    both = [jnp.concatenate([er, ei], 1).astype(jnp.bfloat16), jnp.concatenate([-ei, er], 1).astype(jnp.bfloat16)]
    zero = jnp.zeros((HALF, LANES), jnp.bfloat16)
    for parity in range(2):
        for kind in range(2):
            for c in range(2):
                at = 2 * kind + flip(parity, c)
                line = [both[kind], zero] if c == 0 else [zero, both[kind]]
                mats[2 * LEVELS + parity, at * HALF:(at + 1) * HALF] = jnp.concatenate(line, 1)


def times(a, b):
    return a[0] * b[0] - a[1] * b[1], a[0] * b[1] + a[1] * b[0]


def wave(weights, codes, mats, put, re, im, powers):
    low = lax.broadcasted_iota(jnp.int32, (ROWS, LANES), 1) < HALF
    high = jnp.logical_not(low)
    flat = lambda tiles: jnp.concatenate(tiles, 0)

    def phase(level, parity, v):
        load = lambda i: (powers[i, 0, parity, v], powers[i, 1, parity, v])

        def keep(i, value):
            powers[i, 0, parity, v], powers[i, 1, parity, v] = value
            return value

        if level == 0:
            angle = jnp.log2(codes(owner(parity, v)).astype(jnp.float32)) * (1.0 / SCALE)
            sine, cosine = sine_cosine(angle)
            return keep(0, (cosine, sine))
        if level == 1:
            cosine, sine = load(0)
            twice = 2.0 * sine
            return keep(1, (1.0 - twice * sine, twice * cosine))
        if level == 2:
            return keep(2, times(load(1), load(0)))
        if level == 3:
            cosine, sine = load(1)
            twice = 2.0 * sine
            return keep(3, (1.0 - twice * sine, twice * cosine))
        if level == 7:
            cosine, sine = load(3)
            twice = 2.0 * sine
            return 1.0 - twice * sine, twice * cosine
        return times(load(3), load(level - 4))

    def rotate_store(mixed, parity, vs, level):
        for k, v in enumerate(vs):
            real = mixed[k * ROWS:(k + 1) * ROWS, :LANES]
            imag = mixed[k * ROWS:(k + 1) * ROWS, LANES:]
            cosine, sine = phase(level, parity, v)
            re[parity, v] = (real * cosine - imag * sine).astype(jnp.bfloat16)
            im[parity, v] = (real * sine + imag * cosine).astype(jnp.bfloat16)

    for blk in range(HALVES // SPAN):
        vs = range(blk * SPAN, (blk + 1) * SPAN)
        for parity in range(2):
            left = [weights((odd_bits(v) + parity) % 2, 2 * v) for v in vs]
            right = [weights((odd_bits(v) + parity) % 2, 2 * v + 1) for v in vs]
            x = jnp.concatenate([flat(left), flat(right)], 1)
            mixed = jnp.dot(x, mats[parity], preferred_element_type=jnp.float32)
            rotate_store(mixed, parity, vs, 0)

    for level in range(1, LEVELS):
        bit = level % 7 - 1
        step = 0 if bit < 0 else 1 << bit
        for blk in range(HALVES // SPAN):
            vs = list(range(blk * SPAN, (blk + 1) * SPAN))
            ws = [v ^ step for v in vs]
            pieces = [[[], []], [[], []]]
            for v, w in zip(vs, ws):
                second = odd_bits(v) if bit < 0 else v >> bit & 1
                mask = high if second else low
                for kind, ref in enumerate((re, im)):
                    even, odd = ref[0, v], ref[1, w]
                    pieces[0][kind].append(jnp.where(mask, even, odd))
                    pieces[1][kind].append(jnp.where(mask, odd, even))
            for parity in range(2):
                x = jnp.concatenate([flat(pieces[parity][0]), flat(pieces[parity][1])], 1)
                mixed = jnp.dot(x, mats[2 * level + parity], preferred_element_type=jnp.float32)
                rotate_store(mixed, parity, (vs, ws)[parity], level)

    for blk in range(HALVES // SPAN):
        vs = range(blk * SPAN, (blk + 1) * SPAN)
        for parity in range(2):
            x = jnp.concatenate([flat([re[parity, v] for v in vs]), flat([im[parity, v] for v in vs])], 1)
            image = jnp.dot(x, mats[2 * LEVELS + parity], preferred_element_type=jnp.float32).astype(jnp.bfloat16)
            for i, v in enumerate(vs):
                for s in range(2):
                    put(s, owner(parity, v), image[i * ROWS:(i + 1) * ROWS, s * LANES:(s + 1) * LANES])


def kernel(
    weights, travel, interp_real, interp_imag, eval_real, eval_imag, image,
    held, coded, angles, reals, imags, er, ei, mats, re, im, powers,
    send_sem, recv_sem, load_sem,
):
    gx, gy = lax.axis_index("gx"), lax.axis_index("gy")
    xh, z, y, u = gx // 4, gx % 4, gy // 4, gy % 4
    bits = xh + z + z // 2 + y + y // 2 + u + u // 2
    odd = bits % 2

    loads = [
        pltpu.make_async_copy(travel.at[:, pl.ds(0, 8192)], angles.at[odd], load_sem.at[0]),
        pltpu.make_async_copy(travel.at[:, pl.ds(8192, 8192)], angles.at[1 - odd], load_sem.at[1]),
        pltpu.make_async_copy(interp_real, reals, load_sem.at[2]),
        pltpu.make_async_copy(interp_imag, imags, load_sem.at[3]),
        pltpu.make_async_copy(eval_real, er, load_sem.at[4]),
        pltpu.make_async_copy(eval_imag, ei, load_sem.at[5]),
    ]
    for load in loads:
        load.start()

    def peer(axis, k):
        if axis == "x":
            p = (xh * 4 + u + k) % 8
            return (p // 4, p % 4), (p // 4 * 4 + z, y * 4 + p % 4)
        if axis == "y":
            p = (y + k) % 4
            return (p,), (gx, p * 4 + u)
        p = (z + k) % 4
        return (p,), (xh * 4 + p, gy)

    def part(axis, at):
        if axis == "x":
            return at[0], slice(None), slice(None), at[1]
        if axis == "y":
            return slice(None), slice(None), at[0]
        return slice(None), at[0]

    def count(axis):
        return 8 if axis == "x" else 4

    barrier = pltpu.get_barrier_semaphore()
    for axis in "xyz":
        def greet(k, _, axis=axis):
            pl.semaphore_signal(barrier, inc=1, device_id=peer(axis, k)[1], device_id_type=MESH)
            return 0
        lax.fori_loop(1, count(axis), greet, 0)
    pl.semaphore_wait(barrier, 13)

    def start(stage, stream, w):
        axis = ORDERS[w][stream][stage]
        if stage > 0:
            source = lambda at: held.at[(stage - 1, stream, w) + part(axis, at)]
        elif stream == CODES:
            source = lambda at: coded.at[(w,) + part(axis, at)]
        else:
            def source(at):
                index = part(axis, at)
                index = index + (slice(None),) * (4 - len(index))
                return weights.at[(stream,) + index + (pl.ds(w * ROWS, ROWS),)]
        mine = peer(axis, 0)[0]
        target = held.at[(stage, stream, w) + part(axis, mine)]

        def send(k, _):
            at, device = peer(axis, k)
            pltpu.make_async_remote_copy(
                src_ref=source(at), dst_ref=target,
                send_sem=send_sem.at[stage, stream, w], recv_sem=recv_sem.at[stage, stream, w],
                device_id=device, device_id_type=MESH,
            ).start()
            return 0

        lax.fori_loop(1, count(axis), send, 0)
        pltpu.make_async_copy(source(mine), target, recv_sem.at[stage, stream, w]).start()

    def land(stage, stream, w):
        whole = held.at[stage, stream, w]
        pltpu.make_async_copy(whole, whole, recv_sem.at[stage, stream, w]).wait()

    for w in range(2):
        for stream in range(2):
            start(0, stream, w)

    loads[0].wait()
    loads[1].wait()

    def encode(hz, _):
        for low in range(8):
            at = pl.ds(pl.multiple_of((hz * 8 + low) * LANES, LANES), LANES)
            both = jnp.concatenate([angles[0, :, at], angles[1, :, at]], 0)
            code = jnp.exp2(SCALE * both).T.astype(jnp.bfloat16)
            for h in range(2):
                for w in range(WAVES):
                    row = h * 64 + w * ROWS
                    coded[w, hz // 4, hz % 4, low // 2, low % 2 * 2 + h] = code[row:row + ROWS]
        return 0

    lax.fori_loop(0, 8, encode, 0)
    for w in range(2):
        start(0, CODES, w)

    streams = range(3)
    for stream in streams:
        land(0, stream, 0)
        start(1, stream, 0)
    for stream in streams:
        land(0, stream, 1)
        start(1, stream, 1)
    for w in range(2):
        for stream in streams:
            land(1, stream, w)
            start(2, stream, w)
        for stream in streams:
            start(0, stream, w + 2)
    for load in loads[2:]:
        load.wait()
    build_matrices(reals, imags, er, ei, mats)

    def step(w, _):
        for stream in streams:
            whole = held.at[2, stream, w]
            pltpu.make_async_copy(whole, whole, recv_sem.at[2, stream, w]).wait()

        def put(s, d, value):
            image[s, d, pl.ds(pl.multiple_of(w * ROWS, ROWS), ROWS)] = value

        wave(
            lambda s, d: held[(2, s, w) + digits(d)], lambda d: held[(2, CODES, w) + digits(d)],
            mats, put, re, im, powers,
        )

        @pl.when(w == 0)
        def _():
            for stream in streams:
                land(0, stream, 2)
                start(1, stream, 2)

        @pl.when(w == 1)
        def _():
            for stream in streams:
                land(0, stream, 3)
                start(1, stream, 3)
            for later in (2, 3):
                for stream in streams:
                    land(1, stream, later)
                    start(2, stream, later)
        return 0

    lax.fori_loop(0, WAVES, step, 0)

    for w in range(WAVES):
        for stream in streams:
            for stage in range(3):
                sent = GROUPS - GROUPS // count(ORDERS[w][stream][stage])
                bytes_of = image.at[0, pl.ds(0, sent), pl.ds(0, ROWS)]
                pltpu.make_async_copy(bytes_of, bytes_of, send_sem.at[stage, stream, w]).wait()


def local(weights, travel, interp_real, interp_imag, eval_real, eval_imag):
    pair_rows, width = weights.shape
    block_rows = pair_rows // (2 * GROUPS)
    bf16, f32 = jnp.bfloat16, jnp.float32
    image = pl.pallas_call(
        kernel,
        in_specs=[pl.BlockSpec(memory_space=pl.ANY)] * 6,
        out_specs=pl.BlockSpec(memory_space=pltpu.VMEM),
        out_shape=pltpu.VMEM((2, GROUPS, block_rows, width), bf16),
        scratch_shapes=[
            pltpu.VMEM((3, 3, WAVES) + DIGITS + (ROWS, LANES), bf16),
            pltpu.VMEM((WAVES,) + DIGITS + (ROWS, LANES), bf16),
            pltpu.VMEM((2, HALF, pair_rows // 2), f32),
            pltpu.VMEM(interp_real.shape, bf16),
            pltpu.VMEM(interp_imag.shape, bf16),
            pltpu.VMEM(eval_real.shape, bf16),
            pltpu.VMEM(eval_imag.shape, bf16),
            pltpu.VMEM((2 * LEVELS + 2, 2 * LANES, 2 * LANES), bf16),
            pltpu.VMEM((2, HALVES, ROWS, LANES), bf16),
            pltpu.VMEM((2, HALVES, ROWS, LANES), bf16),
            pltpu.VMEM((4, 2, 2, HALVES, ROWS, LANES), f32),
            pltpu.SemaphoreType.DMA((3, 3, WAVES)),
            pltpu.SemaphoreType.DMA((3, 3, WAVES)),
            pltpu.SemaphoreType.DMA((6,)),
        ],
        compiler_params=pltpu.CompilerParams(
            collective_id=0, has_side_effects=True, vmem_limit_bytes=56 << 20
        ),
    )(weights.reshape((2,) + DIGITS + (block_rows, width)), travel.T, interp_real, interp_imag, eval_real, eval_imag)
    return image.reshape(pair_rows, width)


def solution(mesh):
    return jax.shard_map(
        local,
        mesh=mesh,
        in_specs=(P(("gx", "gy"), None), P(("gx", "gy"), None), P(), P(), P(), P()),
        out_specs=P(("gx", "gy"), None),
        check_vma=False,
    )
```

time: 586 us -> 88.1 us (0.15); the launches traced: 577 us -> 88 us
  waiting for transfers between devices: 320 us -> 0 us
  other arithmetic: 132 us -> 0 us
  Pallas kernels: 0 us -> 86 us
  local copies, waits for them, and re-layouts: 65.6 us -> 2.02 us
  starting transfers between devices: 30 us -> 0 us
  matrix products: 28.6 us -> 0 us
    ppermute x8 -> x0, waiting for transfers between devices: 268 us -> none  [from_partner(): lax.ppermute(x, axis, [(i, i ^ 1 << stride) for i in range(lax.axis_size(...]
    another operation x8 -> x0, other arithmetic: 113 us -> none
    pallas_call x0 -> x1, Pallas kernels: none -> 86 us  [local(): pl.pallas_call(kernel, in_specs=[pl.BlockSpec(memory_space=pl.ANY)] * 6,...]
    all_to_all x1 -> x0, waiting for transfers between devices: 52.4 us -> none  [local(): lax.all_to_all(state.reshape(2, groups, block_rows, width), ('gx', 'gy'),...]
    dot_general x9 -> x0, matrix products: 28.6 us -> none  [the longest x8 25.2 us: local(): mixed = jnp.dot(paired, matrix, preferred_element_type=jnp.float32)]
    concatenate x3 -> x0, local copies, waits for them, and re-layouts: 23.6 us -> none  [rotate(): jnp.concatenate([real_part * cosine - imag_part * sine, real_part * sine...]
    ppermute x8 -> x0, starting transfers between devices: 20.1 us -> none  [from_partner(): lax.ppermute(x, axis, [(i, i ^ 1 << stride) for i in range(lax.axis_size(...]
    concatenate x8 -> x0, other arithmetic: 18.5 us -> none  [rotate(): jnp.concatenate([real_part * cosine - imag_part * sine, real_part * sine...]
  transfers between devices with their start and end apart: 9 -> 0, of which waited for: 8 -> 0; matrix products, arithmetic and copies ran while one was open for 3% -> 0% of each run, Pallas kernels for 0% -> 0%
where the time goes in v2:
time: 88.1 us; the launch traced here: 88 us
  Pallas kernels  86 us (98%)
  local copies, waits for them, and re-layouts  2.02 us (2%)
    pallas_call x1, Pallas kernels, local(): pl.pallas_call(kernel, in_specs=[pl.BlockSpec(memory_space=pl.ANY)] * 6,...  86 us
    unnamed x1, local copies, waits for them, and re-layouts  2.02 us

profile of v2, /device:TPU:1, one launch (start us, length us, event | category | flops | bytes accessed | tf_op | source)
XLA Modules:
  0.0 88.0 jit_solution(11623533701616783143)
XLA Ops:
  0.0 86.0 %shard_map.64 = bf16[2,128,64,128]{3,2,1,0:T(8,128)(2,1)S(1)} custom-call(bf16[2,2,4,4,4,64,128]{6,5,4,3,2,1,0:T(8,128)(2,1)} %bitcast.4, f32[64,16384]{1,0:T(8,128)} %bitcast.5, bf16[8,2,2,64,64]{4,3,2,1,0:T(8,128)(2,1)} %interp_real.1, bf16[8,2,2,64,64]{4,3,2,1,0:T(8,128)(2,1)} %interp_imag.1, bf16[64,64]{1,0:T(8,128)(2,1)} %eval_real.1, ...), custom_call_target="tpu_custom_call" | custom-call | tf_op jit(solution)/shard_map/pallas_call | solution.py:333
  86.0 2.0 %copy.8 = bf16[16384,128]{1,0:T(8,128)(2,1)} copy(bf16[16384,128]{1,0:T(8,128)(2,1)S(1)} %bitcast.3) | data formatting | bytes 8388608

commit v3 on v2

v3 whole, which is shorter than its diff:
```python
import functools

import jax
import jax.numpy as jnp
from jax import lax
from jax.experimental import pallas as pl
from jax.experimental.pallas import tpu as pltpu
from jax.sharding import PartitionSpec as P

MESH = pl.DeviceIdType.MESH
LEVELS = 8
GROUPS = 128
HALVES = GROUPS // 2
ROWS = 16
WAVES = 4
LANES = 128
HALF = LANES // 2
SPAN = 16
SCALE = 40.0
DECODE = 0.018033688011112043
DIGITS = (2, 4, 4, 4)
CODES = 2
GROUPED = (
    ((0, 0), (1, 0), (2, 0)),
    ((2, 1), (2, 2), (2, 3)),
    ((0, 1), (1, 1), (0, 2)),
    ((1, 2), (0, 3), (1, 3)),
)
SLOTS = 3


def axis_of(place, stage):
    return "xyz"[(place + stage) % 3]


def odd_bits(n):
    return bin(n).count("1") % 2


def digits(d):
    return d // 64, d // 16 % 4, d // 4 % 4, d % 4


def double(a):
    twice = a[1] + a[1]
    return 1.0 - twice * a[1], twice * a[0]


def next_odd(twice, even, odd):
    return twice * even[0] - odd[0], twice * even[1] - odd[1]


def unit(half):
    sq = half * half
    sine = half * (0.999999977 + sq * (-1.66666476e-1 + sq * (8.33289965e-3 + sq * (-1.98008872e-4 + sq * 2.59046704e-6))))
    cosine = 0.99999995 + sq * (-0.49999905 + sq * (4.16635835e-2 + sq * (-1.38536951e-3 + sq * 2.3153718e-5)))
    return double((cosine, sine))


def build_matrices(real, imag, eval_real, eval_imag, mats):
    flip = lambda parity, child: (child + parity) % 2

    def blocks_of(level):
        tr = [[real[level, c, e].astype(jnp.float32).T for e in range(2)] for c in range(2)]
        ti = [[imag[level, c, e].astype(jnp.float32).T for e in range(2)] for c in range(2)]

        def rows(kind, e, parity):
            a, b = flip(parity, 0), flip(parity, 1)
            if kind == 0:
                parts = [tr[a][e], tr[b][e], ti[a][e], ti[b][e]]
            else:
                parts = [-ti[a][e], -ti[b][e], tr[a][e], tr[b][e]]
            return jnp.concatenate(parts, 1).astype(jnp.bfloat16)

        return rows

    rows = blocks_of(0)
    for parity in range(2):
        for e in range(2):
            for kind in range(2):
                mats[parity, (2 * e + kind) * HALF:(2 * e + kind + 1) * HALF] = rows(kind, e, parity)

    def level_body(level, _):
        rows = blocks_of(level)
        for parity in range(2):
            for kind in range(2):
                for e in range(2):
                    at = 2 * kind + flip(parity, e)
                    mats[2 * level + parity, at * HALF:(at + 1) * HALF] = rows(kind, e, parity)
        return 0

    lax.fori_loop(1, LEVELS, level_body, 0)
    er = eval_real[...].astype(jnp.float32).T
    ei = eval_imag[...].astype(jnp.float32).T
    both = [jnp.concatenate([er, ei], 1).astype(jnp.bfloat16), jnp.concatenate([-ei, er], 1).astype(jnp.bfloat16)]
    zero = jnp.zeros((HALF, LANES), jnp.bfloat16)
    for parity in range(2):
        for kind in range(2):
            for c in range(2):
                at = 2 * kind + flip(parity, c)
                line = [both[kind], zero] if c == 0 else [zero, both[kind]]
                mats[2 * LEVELS + parity, at * HALF:(at + 1) * HALF] = jnp.concatenate(line, 1)


def tables(codes, powers):
    def body(blk, _):
        turn = lax.rem(blk + blk // 2 + blk // 4, 2)
        for s in range(2):
            for parity in range(2):
                for y in range(4):
                    k = blk * 4 + y
                    e = odd_bits(y) ^ parity ^ s
                    u = 2 * (e + turn * (1 - 2 * e)) + s
                    one = unit(jnp.log(codes(blk, y, u).astype(jnp.float32)) * DECODE)
                    twice = one[0] + one[0]
                    two = double(one)
                    three = next_odd(twice, two, one)
                    four = double(two)
                    five = next_odd(twice, four, three)
                    six = double(three)
                    all_powers = (one, two, three, four, five, six, next_odd(twice, six, five), double(four))
                    for n, value in enumerate(all_powers):
                        for i in range(2):
                            powers[n, i, s, parity, k] = value[i].astype(jnp.bfloat16)
        return 0

    lax.fori_loop(0, 8, body, 0)


def rotate(mixed, powers, level, at, re, im):
    mixed = mixed.astype(jnp.bfloat16)
    real = mixed[:, :LANES].reshape(SPAN, ROWS, LANES)
    imag = mixed[:, LANES:].reshape(SPAN, ROWS, LANES)
    cosine, sine = powers[(level, 0) + at], powers[(level, 1) + at]
    re[at] = real * cosine - imag * sine
    im[at] = real * sine + imag * cosine


def low_lanes(tiles=None):
    shape = (ROWS, LANES) if tiles is None else (tiles, ROWS, LANES)
    return lax.broadcasted_iota(jnp.int32, shape, len(shape) - 1) < HALF


def flat(tiles):
    return jnp.concatenate(tiles, 0)


def rows(tiles):
    return tiles.reshape(SPAN * ROWS, LANES)


def multiply(real, imag, matrix):
    return jnp.dot(jnp.concatenate([real, imag], 1), matrix, preferred_element_type=jnp.float32)


def combine(even, odd, take, mats, level, powers, re, im):
    pieces = [take(ref[even], ref[odd]) for ref in (re, im)]
    for parity, at in enumerate((even, odd)):
        mixed = multiply(rows(pieces[0][parity]), rows(pieces[1][parity]), mats[2 * level + parity])
        rotate(mixed, powers, level, at, re, im)


def swap(mask):
    return lambda even, odd: (jnp.where(mask, even, odd), jnp.where(mask, odd, even))


def halves(tiles, step):
    parts = tiles.reshape(SPAN // (2 * step), 2, step, ROWS, LANES)
    return [parts[:, n].reshape(SPAN // 2, ROWS, LANES) for n in range(2)]


def whole(parts, step):
    shape = (SPAN // (2 * step), 1, step, ROWS, LANES)
    return jnp.concatenate([p.reshape(shape) for p in parts], 1).reshape(SPAN, ROWS, LANES)


def swap_across(step, low):
    def take(even, odd):
        high = jnp.logical_not(low)
        even, odd = halves(even, step), halves(odd, step)
        return (
            whole([jnp.where(low, even[0], odd[1]), jnp.where(high, even[1], odd[0])], step),
            whole([jnp.where(high, odd[0], even[1]), jnp.where(low, odd[1], even[0])], step),
        )

    return take


def chain(s, weights, mats, powers, re, im):
    low = low_lanes()
    if isinstance(s, int):
        turned = jnp.logical_not(low) if s else low
    else:
        turned = jnp.logical_xor(low, jnp.broadcast_to(s == 1, low.shape))
    starts = range(0, GROUPS // 4, SPAN)
    span = lambda at: pl.ds(at, SPAN)

    def first():
        for at in starts:
            for parity in range(2):
                left, right = [], []
                for k in range(at, at + SPAN):
                    bit = s if odd_bits(k) ^ parity == 0 else 1 - s
                    left.append(weights(k // 4, k % 4, 2 * bit))
                    right.append(weights(k // 4, k % 4, 2 * bit + 1))
                rotate(multiply(flat(left), flat(right), mats[parity]), powers, 0, (s, parity, span(at)), re, im)

    def later(level):
        step = 1 << level - 2 if level > 1 else 0

        def second(even, odd):
            masks = [jnp.logical_not(turned) if odd_bits(k) else turned for k in range(SPAN)]
            if starts_odd:
                masks = [jnp.logical_not(m) for m in masks]
            return (
                jnp.stack([jnp.where(m, even[k], odd[k]) for k, m in enumerate(masks)]),
                jnp.stack([jnp.where(m, odd[k], even[k]) for k, m in enumerate(masks)]),
            )

        for at in starts:
            starts_odd = odd_bits(at)
            if level == 1:
                take = second
            elif step < SPAN:
                take = swap_across(step, low_lanes(SPAN // 2))
            else:
                wide = low_lanes(SPAN)
                take = swap(jnp.logical_not(wide) if at & step else wide)
            other = at ^ step if step >= SPAN else at
            combine((s, 0, span(at)), (s, 1, span(other)), take, mats, level, powers, re, im)

    return [first] + [functools.partial(later, level) for level in range(1, LEVELS - 1)]


def together(*chains):
    for levels in zip(*chains):
        for level in levels:
            level()


def joint(mats, powers, re, im, put):
    low = low_lanes(SPAN)
    for s in range(2):
        take = swap(jnp.logical_not(low) if s else low)
        for at in range(0, GROUPS // 4, SPAN):
            ks = pl.ds(at, SPAN)
            combine((s, 0, ks), (1 - s, 1, ks), take, mats, LEVELS - 1, powers, re, im)
    for s in range(2):
        for parity in range(2):
            for at in range(0, GROUPS // 4, SPAN):
                place = (s, parity, pl.ds(at, SPAN))
                image = multiply(rows(re[place]), rows(im[place]), mats[2 * LEVELS + parity]).astype(jnp.bfloat16)
                for n in range(SPAN):
                    k = at + n
                    for c in range(2):
                        put(
                            c, 4 * k + 2 * (odd_bits(k) ^ parity ^ s) + s,
                            image[n * ROWS:(n + 1) * ROWS, c * LANES:(c + 1) * LANES],
                        )


def kernel(
    weights, travel, interp_real, interp_imag, eval_real, eval_imag, image,
    held, coded, angles, reals, imags, er, ei, mats, re, im, powers,
    send_sem, recv_sem, load_sem,
):
    gx, gy = lax.axis_index("gx"), lax.axis_index("gy")
    xh, z, y, u = gx // 4, gx % 4, gy // 4, gy % 4
    bits = xh + z + z // 2 + y + y // 2 + u + u // 2
    odd = bits % 2

    loads = [
        pltpu.make_async_copy(travel.at[:, pl.ds(0, 8192)], angles.at[odd], load_sem.at[0]),
        pltpu.make_async_copy(travel.at[:, pl.ds(8192, 8192)], angles.at[1 - odd], load_sem.at[1]),
        pltpu.make_async_copy(interp_real, reals, load_sem.at[2]),
        pltpu.make_async_copy(interp_imag, imags, load_sem.at[3]),
        pltpu.make_async_copy(eval_real, er, load_sem.at[4]),
        pltpu.make_async_copy(eval_imag, ei, load_sem.at[5]),
    ]
    for load in loads:
        load.start()

    def peer(axis, k):
        if axis == "x":
            x = (xh * 2 + u // 2 + k // 2) % 4
            to = x % 2 * 2 + (u + k) % 2
            return (x // 2, to), (x // 2 * 4 + z, y * 4 + to)
        if axis == "y":
            p = (y + k) % 4
            return (p,), (gx, p * 4 + u)
        p = (z + k) % 4
        return (p,), (xh * 4 + p, gy)

    def part(axis, at):
        if axis == "x":
            return at[0], slice(None), slice(None), at[1]
        if axis == "y":
            return slice(None), slice(None), at[0]
        return slice(None), at[0]

    def count(axis):
        return 8 if axis == "x" else 4

    barrier = pltpu.get_barrier_semaphore()
    for axis in "xyz":
        def greet(k, _, axis=axis):
            pl.semaphore_signal(barrier, inc=1, device_id=peer(axis, k)[1], device_id_type=MESH)
            return 0
        lax.fori_loop(1, count(axis), greet, 0)
    pl.semaphore_wait(barrier, 13)

    def go(group, stage):
        items = GROUPED[group]
        sends = {}
        for place, (stream, w) in enumerate(items):
            if stage > 0:
                land(stage - 1, stream, w)
            sends[axis_of(place, stage)] = one(stage, stream, w, axis_of(place, stage))

        def send(i, _):
            k = 2 + i - i // 2 * 3
            sends["x"][0](2 * k)
            sends["y"][0](k)
            sends["z"][0](k)
            sends["x"][0](2 * k + 1)
            return 0

        lax.fori_loop(0, 3, send, 0)
        sends["x"][0](1)
        for axis in "xyz":
            sends[axis][1]()

    def one(stage, stream, w, axis):
        if stage > 0:
            source = lambda at: held.at[(stage - 1, stream, w) + part(axis, at)]
        elif stream == CODES:
            source = lambda at: coded.at[(w,) + part(axis, at)]
        else:
            def source(at):
                index = part(axis, at)
                index = index + (slice(None),) * (4 - len(index))
                return weights.at[(stream,) + index + (pl.ds(w * ROWS, ROWS),)]
        mine = peer(axis, 0)[0]
        target = held.at[(stage, stream, w) + part(axis, mine)]

        def send(k):
            at, device = peer(axis, k)
            pltpu.make_async_remote_copy(
                src_ref=source(at), dst_ref=target,
                send_sem=send_sem.at[stage, stream, w], recv_sem=recv_sem.at[stage, stream, w],
                device_id=device, device_id_type=MESH,
            ).start()

        def keep():
            pltpu.make_async_copy(source(mine), target, recv_sem.at[stage, stream, w]).start()

        return send, keep

    def land(stage, stream, w):
        whole = held.at[stage, stream, w]
        pltpu.make_async_copy(whole, whole, recv_sem.at[stage, stream, w]).wait()

    go(2, 0)
    go(3, 0)

    loads[0].wait()
    loads[1].wait()

    def encode(hz, _):
        for low in range(8):
            at = pl.ds(pl.multiple_of((hz * 8 + low) * LANES, LANES), LANES)
            both = jnp.concatenate([angles[0, :, at], angles[1, :, at]], 0)
            code = jnp.exp2(SCALE * both).astype(jnp.bfloat16).T
            for h in range(2):
                for w in range(WAVES):
                    row = h * 64 + w * ROWS
                    coded[w, hz // 4, hz % 4, low // 2, low % 2 * 2 + h] = code[row:row + ROWS]
        return 0

    lax.fori_loop(0, 8, encode, 0)
    go(0, 0)
    go(1, 0)
    go(0, 1)
    go(1, 1)
    go(0, 2)
    for load in loads[2:]:
        load.wait()
    build_matrices(reals, imags, er, ei, mats)
    go(1, 2)
    go(2, 1)
    go(3, 1)

    def tabulate(w):
        land(2, CODES, w)
        tables(lambda blk, y, u: held[2, CODES, w, blk // 4, blk % 4, y, u], powers.at[w % SLOTS])

    tabulate(0)

    def links(s, w, state):
        return chain(
            s, lambda xz, y, u: held[2, s, w, xz // 4, xz % 4, y, u], mats, powers.at[w % SLOTS], *state
        )

    def finish(w, state):
        def put(c, d, value):
            image[c, d, pl.ds(pl.multiple_of(w * ROWS, ROWS), ROWS)] = value

        joint(mats, powers.at[w % SLOTS], *state, put)

    near, far = (re.at[0], im.at[0]), (re.at[1], im.at[1])
    land(2, 0, 0)
    land(2, 1, 0)

    def side(s, _):
        together(links(s, 0, near))
        return 0

    lax.fori_loop(0, 2, side, 0)
    finish(0, near)
    tabulate(1)
    go(2, 2)
    tabulate(2)
    go(3, 2)
    tabulate(3)

    def step(t, _):
        w = 1 + 2 * t
        land(2, 0, w)
        land(2, 1, w)
        land(2, t, 2)
        together(links(0, w, near), links(1, w, near), links(t, 2, far))
        finish(w, near)
        return 0

    lax.fori_loop(0, 2, step, 0)
    finish(2, far)

    for items in GROUPED:
        for place, (stream, w) in enumerate(items):
            for stage in range(3):
                sent = GROUPS - GROUPS // count(axis_of(place, stage))
                bytes_of = image.at[0, pl.ds(0, sent), pl.ds(0, ROWS)]
                pltpu.make_async_copy(bytes_of, bytes_of, send_sem.at[stage, stream, w]).wait()


def local(weights, travel, interp_real, interp_imag, eval_real, eval_imag):
    pair_rows, width = weights.shape
    block_rows = pair_rows // (2 * GROUPS)
    bf16, f32 = jnp.bfloat16, jnp.float32
    image = pl.pallas_call(
        kernel,
        in_specs=[pl.BlockSpec(memory_space=pl.ANY)] * 6,
        out_specs=pl.BlockSpec(memory_space=pltpu.VMEM),
        out_shape=pltpu.VMEM((2, GROUPS, block_rows, width), bf16),
        scratch_shapes=[
            pltpu.VMEM((3, 3, WAVES) + DIGITS + (ROWS, LANES), bf16),
            pltpu.VMEM((WAVES,) + DIGITS + (ROWS, LANES), bf16),
            pltpu.VMEM((2, HALF, pair_rows // 2), f32),
            pltpu.VMEM(interp_real.shape, bf16),
            pltpu.VMEM(interp_imag.shape, bf16),
            pltpu.VMEM(eval_real.shape, bf16),
            pltpu.VMEM(eval_imag.shape, bf16),
            pltpu.VMEM((2 * LEVELS + 2, 2 * LANES, 2 * LANES), bf16),
            pltpu.VMEM((2, 2, 2, GROUPS // 4, ROWS, LANES), bf16),
            pltpu.VMEM((2, 2, 2, GROUPS // 4, ROWS, LANES), bf16),
            pltpu.VMEM((SLOTS, LEVELS, 2, 2, 2, GROUPS // 4, ROWS, LANES), bf16),
            pltpu.SemaphoreType.DMA((3, 3, WAVES)),
            pltpu.SemaphoreType.DMA((3, 3, WAVES)),
            pltpu.SemaphoreType.DMA((6,)),
        ],
        compiler_params=pltpu.CompilerParams(
            collective_id=0, has_side_effects=True, vmem_limit_bytes=56 << 20
        ),
    )(weights.reshape((2,) + DIGITS + (block_rows, width)), travel.T, interp_real, interp_imag, eval_real, eval_imag)
    return image.reshape(pair_rows, width)


def solution(mesh):
    return jax.shard_map(
        local,
        mesh=mesh,
        in_specs=(P(("gx", "gy"), None), P(("gx", "gy"), None), P(), P(), P(), P()),
        out_specs=P(("gx", "gy"), None),
        check_vma=False,
    )
```

time: 88.1 us -> 87.1 us (0.989)
  Pallas kernels: 86 us -> 84.6 us
    pallas_call x1, Pallas kernels: 86 us -> 84.6 us  [local(): pl.pallas_call(kernel, in_specs=[pl.BlockSpec(memory_space=pl.ANY)] * 6,...]
where the time goes in v3:
time: 87.1 us; the launch traced here: 86.7 us
  Pallas kernels  84.6 us (97%)
  local copies, waits for them, and re-layouts  2.02 us (2%)
    pallas_call x1, Pallas kernels, local(): pl.pallas_call(kernel, in_specs=[pl.BlockSpec(memory_space=pl.ANY)] * 6,...  84.6 us
    unnamed x1, local copies, waits for them, and re-layouts  2.02 us

profile of v3, /device:TPU:1, one launch (start us, length us, event | category | flops | bytes accessed | tf_op | source)
XLA Modules:
  0.0 86.7 jit_solution(7296900141597112960)
XLA Ops:
  0.0 84.6 %shard_map.64 = bf16[2,128,64,128]{3,2,1,0:T(8,128)(2,1)S(1)} custom-call(bf16[2,2,4,4,4,64,128]{6,5,4,3,2,1,0:T(8,128)(2,1)} %bitcast.4, f32[64,16384]{1,0:T(8,128)} %bitcast.5, bf16[8,2,2,64,64]{4,3,2,1,0:T(8,128)(2,1)} %interp_real.1, bf16[8,2,2,64,64]{4,3,2,1,0:T(8,128)(2,1)} %interp_imag.1, bf16[64,64]{1,0:T(8,128)(2,1)} %eval_real.1, ...), custom_call_target="tpu_custom_call" | custom-call | tf_op jit(solution)/shard_map/pallas_call | solution.py:450
  84.6 2.0 %copy.8 = bf16[16384,128]{1,0:T(8,128)(2,1)} copy(bf16[16384,128]{1,0:T(8,128)(2,1)S(1)} %bitcast.3) | data formatting | bytes 8388608

commit v4 on v3

v4 whole, which is shorter than its diff:
```python
import jax
import jax.numpy as jnp
from jax import lax
from jax.experimental import pallas as pl
from jax.experimental.pallas import tpu as pltpu
from jax.sharding import PartitionSpec as P

MESH = pl.DeviceIdType.MESH
LEVELS = 8
GROUPS = 128
HALVES = GROUPS // 2
ROWS = 16
WAVES = 4
LANES = 128
HALF = LANES // 2
SPAN = 16
SCALE = 40.0
DECODE = 0.018033688011112043
DIGITS = (2, 4, 4, 4)
CODES = 2
GROUPED = (
    ((0, 0), (1, 0), (2, 0)),
    ((2, 1), (2, 2), (2, 3)),
    ((0, 1), (1, 1), (0, 2)),
    ((1, 2), (0, 3), (1, 3)),
)


def axis_of(place, stage):
    return "xyz"[(place + stage) % 3]


def odd_bits(n):
    return bin(n).count("1") % 2


def digits(d):
    return d // 64, d // 16 % 4, d // 4 % 4, d % 4


def double(a):
    twice = a[1] + a[1]
    return 1.0 - twice * a[1], twice * a[0]


def next_odd(twice, even, odd):
    return twice * even[0] - odd[0], twice * even[1] - odd[1]


def unit(half):
    sq = half * half
    sine = half * (0.999999977 + sq * (-1.66666476e-1 + sq * (8.33289965e-3 + sq * (-1.98008872e-4 + sq * 2.59046704e-6))))
    cosine = 0.99999995 + sq * (-0.49999905 + sq * (4.16635835e-2 + sq * (-1.38536951e-3 + sq * 2.3153718e-5)))
    return double((cosine, sine))


def build_matrices(real, imag, eval_real, eval_imag, mats):
    flip = lambda parity, child: (child + parity) % 2

    def halves(level):
        tr = [[real[level, c, e].astype(jnp.float32).T for e in range(2)] for c in range(2)]
        ti = [[imag[level, c, e].astype(jnp.float32).T for e in range(2)] for c in range(2)]

        def rows(kind, e, parity):
            a, b = flip(parity, 0), flip(parity, 1)
            if kind == 0:
                parts = [tr[a][e], tr[b][e], ti[a][e], ti[b][e]]
            else:
                parts = [-ti[a][e], -ti[b][e], tr[a][e], tr[b][e]]
            return jnp.concatenate(parts, 1).astype(jnp.bfloat16)

        return rows

    rows = halves(0)
    for parity in range(2):
        for e in range(2):
            for kind in range(2):
                mats[parity, (2 * e + kind) * HALF:(2 * e + kind + 1) * HALF] = rows(kind, e, parity)

    def level_body(level, _):
        rows = halves(level)
        for parity in range(2):
            for kind in range(2):
                for e in range(2):
                    at = 2 * kind + flip(parity, e)
                    mats[2 * level + parity, at * HALF:(at + 1) * HALF] = rows(kind, e, parity)
        return 0

    lax.fori_loop(1, LEVELS, level_body, 0)
    er = eval_real[...].astype(jnp.float32).T
    ei = eval_imag[...].astype(jnp.float32).T
    both = [jnp.concatenate([er, ei], 1).astype(jnp.bfloat16), jnp.concatenate([-ei, er], 1).astype(jnp.bfloat16)]
    zero = jnp.zeros((HALF, LANES), jnp.bfloat16)
    for parity in range(2):
        for kind in range(2):
            for c in range(2):
                at = 2 * kind + flip(parity, c)
                line = [both[kind], zero] if c == 0 else [zero, both[kind]]
                mats[2 * LEVELS + parity, at * HALF:(at + 1) * HALF] = jnp.concatenate(line, 1)


def tables(codes, powers):
    def body(blk, _):
        turn = lax.rem(blk + blk // 2 + blk // 4, 2)
        for s in range(2):
            for parity in range(2):
                for y in range(4):
                    k = blk * 4 + y
                    e = odd_bits(y) ^ parity ^ s
                    u = 2 * (e + turn * (1 - 2 * e)) + s
                    one = unit(jnp.log(codes(blk, y, u).astype(jnp.float32)) * DECODE)
                    twice = one[0] + one[0]
                    two = double(one)
                    three = next_odd(twice, two, one)
                    four = double(two)
                    five = next_odd(twice, four, three)
                    six = double(three)
                    all_powers = (one, two, three, four, five, six, next_odd(twice, six, five), double(four))
                    for n, value in enumerate(all_powers):
                        for i in range(2):
                            powers[n, i, s, parity, k] = value[i].astype(jnp.bfloat16)
        return 0

    lax.fori_loop(0, 8, body, 0)


def rotate(mixed, powers, level, places, re, im):
    mixed = mixed.astype(jnp.bfloat16)
    for n, at in enumerate(places):
        real = mixed[n * ROWS:(n + 1) * ROWS, :LANES]
        imag = mixed[n * ROWS:(n + 1) * ROWS, LANES:]
        cosine, sine = powers[(level, 0) + at], powers[(level, 1) + at]
        re[at] = real * cosine - imag * sine
        im[at] = real * sine + imag * cosine


def low_lanes():
    return lax.broadcasted_iota(jnp.int32, (ROWS, LANES), 1) < HALF


def flat(tiles):
    return jnp.concatenate(tiles, 0)


def combine(evens, odds, masks, mats, level, powers, re, im):
    pieces = [[[], []], [[], []]]
    for even, odd, mask in zip(evens, odds, masks):
        for kind, ref in enumerate((re, im)):
            a, b = ref[even], ref[odd]
            pieces[0][kind].append(jnp.where(mask, a, b))
            pieces[1][kind].append(jnp.where(mask, b, a))
    for parity, places in enumerate((evens, odds)):
        x = jnp.concatenate([flat(pieces[parity][0]), flat(pieces[parity][1])], 1)
        mixed = jnp.dot(x, mats[2 * level + parity], preferred_element_type=jnp.float32)
        rotate(mixed, powers, level, places, re, im)


def chain(s, weights, mats, powers, re, im):
    low = low_lanes()
    turned = jnp.logical_xor(low, jnp.broadcast_to(s == 1, low.shape))
    blocks = [range(at, at + SPAN) for at in range(0, GROUPS // 4, SPAN)]
    for ks in blocks:
        for parity in range(2):
            left, right = [], []
            for k in ks:
                bit = s if odd_bits(k) ^ parity == 0 else 1 - s
                left.append(weights(k // 4, k % 4, 2 * bit))
                right.append(weights(k // 4, k % 4, 2 * bit + 1))
            x = jnp.concatenate([flat(left), flat(right)], 1)
            mixed = jnp.dot(x, mats[parity], preferred_element_type=jnp.float32)
            rotate(mixed, powers, 0, [(s, parity, k) for k in ks], re, im)
    for level in range(1, LEVELS - 1):
        step = 1 << level - 2 if level > 1 else 0
        for ks in blocks:
            if level > 1:
                masks = [jnp.logical_not(low) if k & step else low for k in ks]
            else:
                masks = [jnp.logical_not(turned) if odd_bits(k) else turned for k in ks]
            combine([(s, 0, k) for k in ks], [(s, 1, k ^ step) for k in ks], masks, mats, level, powers, re, im)


def joint(mats, powers, re, im, put):
    low = low_lanes()
    for at in range(0, HALVES, SPAN):
        vs = range(at, at + SPAN)
        side = [odd_bits(v) for v in vs]
        evens = [(e, 0, v // 2) for e, v in zip(side, vs)]
        odds = [(1 - e, 1, v // 2) for e, v in zip(side, vs)]
        masks = [jnp.logical_not(low) if e else low for e in side]
        combine(evens, odds, masks, mats, LEVELS - 1, powers, re, im)
    for at in range(0, HALVES, SPAN):
        vs = range(at, at + SPAN)
        for parity in range(2):
            places = [(odd_bits(v) ^ parity, parity, v // 2) for v in vs]
            x = jnp.concatenate([flat([re[p] for p in places]), flat([im[p] for p in places])], 1)
            image = jnp.dot(x, mats[2 * LEVELS + parity], preferred_element_type=jnp.float32).astype(jnp.bfloat16)
            for n, v in enumerate(vs):
                for c in range(2):
                    put(c, 2 * v + places[n][0], image[n * ROWS:(n + 1) * ROWS, c * LANES:(c + 1) * LANES])


def kernel(
    weights, travel, interp_real, interp_imag, eval_real, eval_imag,
    image, last, mats, last_powers,
    held, coded, angles, reals, imags, er, ei, powers, re, im, send_sem, recv_sem, load_sem,
):
    gx, gy = lax.axis_index("gx"), lax.axis_index("gy")
    xh, z, y, u = gx // 4, gx % 4, gy // 4, gy % 4
    bits = xh + z + z // 2 + y + y // 2 + u + u // 2
    odd = bits % 2

    def peer(axis, k):
        if axis == "x":
            x = (xh * 2 + u // 2 + k // 2) % 4
            to = x % 2 * 2 + (u + k) % 2
            return (x // 2, to), (x // 2 * 4 + z, y * 4 + to)
        if axis == "y":
            p = (y + k) % 4
            return (p,), (gx, p * 4 + u)
        p = (z + k) % 4
        return (p,), (xh * 4 + p, gy)

    def part(axis, at):
        if axis == "x":
            return at[0], slice(None), slice(None), at[1]
        if axis == "y":
            return slice(None), slice(None), at[0]
        return slice(None), at[0]

    def count(axis):
        return 8 if axis == "x" else 4

    barrier = pltpu.get_barrier_semaphore()
    for axis in "xyz":
        def greet(k, _, axis=axis):
            pl.semaphore_signal(barrier, inc=1, device_id=peer(axis, k)[1], device_id_type=MESH)
            return 0
        lax.fori_loop(1, count(axis), greet, 0)
    loads = [
        pltpu.make_async_copy(travel.at[:, pl.ds(0, 8192)], angles.at[odd], load_sem.at[0]),
        pltpu.make_async_copy(travel.at[:, pl.ds(8192, 8192)], angles.at[1 - odd], load_sem.at[1]),
        pltpu.make_async_copy(interp_real, reals, load_sem.at[2]),
        pltpu.make_async_copy(interp_imag, imags, load_sem.at[3]),
        pltpu.make_async_copy(eval_real, er, load_sem.at[4]),
        pltpu.make_async_copy(eval_imag, ei, load_sem.at[5]),
    ]
    for load in loads:
        load.start()
    pl.semaphore_wait(barrier, 13)

    def go(group, stage):
        items = GROUPED[group]
        sends = {}
        for place, (stream, w) in enumerate(items):
            if stage > 0:
                land(stage - 1, stream, w)
            sends[axis_of(place, stage)] = one(stage, stream, w, axis_of(place, stage))

        def send(i, _):
            k = 2 + i - i // 2 * 3
            sends["x"][0](2 * k)
            sends["y"][0](k)
            sends["z"][0](k)
            sends["x"][0](2 * k + 1)
            return 0

        lax.fori_loop(0, 3, send, 0)
        sends["x"][0](1)
        for axis in "xyz":
            sends[axis][1]()

    def one(stage, stream, w, axis):
        if stage > 0:
            source = lambda at: held.at[(stage - 1, stream, w) + part(axis, at)]
        elif stream == CODES:
            source = lambda at: coded.at[(w,) + part(axis, at)]
        else:
            def source(at):
                index = part(axis, at)
                index = index + (slice(None),) * (4 - len(index))
                return weights.at[(stream,) + index + (pl.ds(w * ROWS, ROWS),)]
        mine = peer(axis, 0)[0]
        target = place_of(stage, stream, w).at[part(axis, mine)]

        def send(k):
            at, device = peer(axis, k)
            pltpu.make_async_remote_copy(
                src_ref=source(at), dst_ref=target,
                send_sem=send_sem.at[stage, stream, w], recv_sem=recv_sem.at[stage, stream, w],
                device_id=device, device_id_type=MESH,
            ).start()

        def keep():
            pltpu.make_async_copy(source(mine), target, recv_sem.at[stage, stream, w]).start()

        return send, keep

    def place_of(stage, stream, w):
        if isinstance(w, int) and (stage, w) == (2, WAVES - 1) and stream != CODES:
            return last.at[stream]
        return held.at[stage, stream, w]

    def land(stage, stream, w):
        place = place_of(stage, stream, w)
        pltpu.make_async_copy(place, place, recv_sem.at[stage, stream, w]).wait()

    go(2, 0)
    go(3, 0)

    loads[0].wait()
    loads[1].wait()

    def encode(hz, _):
        for low in range(8):
            at = pl.ds(pl.multiple_of((hz * 8 + low) * LANES, LANES), LANES)
            both = jnp.concatenate([angles[0, :, at], angles[1, :, at]], 0)
            code = jnp.exp2(SCALE * both).astype(jnp.bfloat16).T
            for h in range(2):
                for w in range(WAVES):
                    row = h * 64 + w * ROWS
                    coded[w, hz // 4, hz % 4, low // 2, low % 2 * 2 + h] = code[row:row + ROWS]
        return 0

    lax.fori_loop(0, 8, encode, 0)
    go(0, 0)
    go(1, 0)
    go(0, 1)
    go(1, 1)
    go(0, 2)
    for load in loads[2:]:
        load.wait()
    build_matrices(reals, imags, er, ei, mats)
    go(1, 2)
    go(2, 1)
    go(3, 1)

    def tabulate(w):
        land(2, CODES, w)
        place = last_powers if w == WAVES - 1 else powers.at[w // 2]
        tables(lambda blk, y, u: held[2, CODES, w, blk // 4, blk % 4, y, u], place)

    tabulate(0)

    def link(n, _):
        s, w = n % 2, n // 2
        land(2, s, w)
        chain(s, lambda xz, y, u: held[2, s, w, xz // 4, xz % 4, y, u], mats, powers.at[w // 2], re, im)

        @pl.when(s == 1)
        def _():
            def put(c, d, value):
                image[w, c, d] = value

            joint(mats, powers.at[w // 2], re, im, put)

        @pl.when(n == 1)
        def _():
            tabulate(1)
            go(2, 2)
            tabulate(2)
            go(3, 2)
            tabulate(3)

        return 0

    lax.fori_loop(0, 2 * (WAVES - 1), link, 0)
    land(2, 0, WAVES - 1)
    land(2, 1, WAVES - 1)

    for items in GROUPED:
        for place, (stream, w) in enumerate(items):
            for stage in range(3):
                sent = GROUPS - GROUPS // count(axis_of(place, stage))
                bytes_of = image.at[0, 0, pl.ds(0, sent)]
                pltpu.make_async_copy(bytes_of, bytes_of, send_sem.at[stage, stream, w]).wait()


def finish(done, last, mats, powers, image, re, im, staged, out_sem):
    def out(source, w):
        return pltpu.make_async_copy(source, image.at[:, :, pl.ds(w * ROWS, ROWS)], out_sem.at[w])

    for w in range(WAVES - 1):
        out(done.at[w], w).start()

    def side(s, _):
        chain(s, lambda xz, y, u: last[s, xz // 4, xz % 4, y, u], mats, powers, re, im)
        return 0

    lax.fori_loop(0, 2, side, 0)

    def put(c, d, value):
        staged[c, d] = value

    joint(mats, powers, re, im, put)
    out(staged, WAVES - 1).start()
    for w in range(WAVES - 1):
        out(done.at[w], w).wait()
    out(staged, WAVES - 1).wait()


def local(weights, travel, interp_real, interp_imag, eval_real, eval_imag):
    pair_rows, width = weights.shape
    block_rows = pair_rows // (2 * GROUPS)
    bf16, f32 = jnp.bfloat16, jnp.float32
    tiles = (2, 2, GROUPS // 4, ROWS, LANES)
    passed = pl.pallas_call(
        kernel,
        in_specs=[pl.BlockSpec(memory_space=pl.ANY)] * 6,
        out_specs=[pl.BlockSpec(memory_space=pltpu.VMEM)] * 4,
        out_shape=[
            pltpu.VMEM((WAVES - 1, 2, GROUPS, ROWS, LANES), bf16),
            pltpu.VMEM((2,) + DIGITS + (ROWS, LANES), bf16),
            pltpu.VMEM((2 * LEVELS + 2, 2 * LANES, 2 * LANES), bf16),
            pltpu.VMEM((LEVELS, 2) + tiles, bf16),
        ],
        scratch_shapes=[
            pltpu.VMEM((3, 3, WAVES) + DIGITS + (ROWS, LANES), bf16),
            pltpu.VMEM((WAVES,) + DIGITS + (ROWS, LANES), bf16),
            pltpu.VMEM((2, HALF, pair_rows // 2), f32),
            pltpu.VMEM(interp_real.shape, bf16),
            pltpu.VMEM(interp_imag.shape, bf16),
            pltpu.VMEM(eval_real.shape, bf16),
            pltpu.VMEM(eval_imag.shape, bf16),
            pltpu.VMEM((2, LEVELS, 2) + tiles, bf16),
            pltpu.VMEM(tiles, bf16),
            pltpu.VMEM(tiles, bf16),
            pltpu.SemaphoreType.DMA((3, 3, WAVES)),
            pltpu.SemaphoreType.DMA((3, 3, WAVES)),
            pltpu.SemaphoreType.DMA((6,)),
        ],
        compiler_params=pltpu.CompilerParams(
            collective_id=0, has_side_effects=True, vmem_limit_bytes=45 << 20
        ),
    )(weights.reshape((2,) + DIGITS + (block_rows, width)), travel.T, interp_real, interp_imag, eval_real, eval_imag)
    image = pl.pallas_call(
        finish,
        in_specs=[pl.BlockSpec(memory_space=pltpu.VMEM)] * 4,
        out_specs=pl.BlockSpec(memory_space=pl.ANY),
        out_shape=pltpu.HBM((2, GROUPS, block_rows, width), bf16),
        scratch_shapes=[
            pltpu.VMEM(tiles, bf16),
            pltpu.VMEM(tiles, bf16),
            pltpu.VMEM((2, GROUPS, ROWS, LANES), bf16),
            pltpu.SemaphoreType.DMA((WAVES,)),
        ],
        compiler_params=pltpu.CompilerParams(vmem_limit_bytes=8 << 20),
    )(*passed)
    return image.reshape(pair_rows, width)


def solution(mesh):
    return jax.shard_map(
        local,
        mesh=mesh,
        in_specs=(P(("gx", "gy"), None), P(("gx", "gy"), None), P(), P(), P(), P()),
        out_specs=P(("gx", "gy"), None),
        check_vma=False,
    )
```

time: 87.1 us -> 84.8 us (0.974)
  local copies, waits for them, and re-layouts: 2.02 us -> 0 us
    pallas_call x1, Pallas kernels: 84.6 us -> 79.7 us  [local(): pl.pallas_call(kernel, in_specs=[pl.BlockSpec(memory_space=pl.ANY)] * 6,...]
    pallas_call x0 -> x1, Pallas kernels: none -> 4.85 us  [local(): pl.pallas_call(finish, in_specs=[pl.BlockSpec(memory_space=pltpu.VMEM)] *...]
    unnamed x1 -> x0, local copies, waits for them, and re-layouts: 2.02 us -> none
where the time goes in v4:
time: 84.8 us; the launch traced here: 84.5 us
  Pallas kernels  84.5 us (100%)
    pallas_call x1, Pallas kernels, local(): pl.pallas_call(kernel, in_specs=[pl.BlockSpec(memory_space=pl.ANY)] * 6,...  79.7 us
    pallas_call x1, Pallas kernels, local(): pl.pallas_call(finish, in_specs=[pl.BlockSpec(memory_space=pltpu.VMEM)] *...  4.85 us

profile of v4, /device:TPU:1, one launch (start us, length us, event | category | flops | bytes accessed | tf_op | source)
XLA Modules:
  0.0 84.5 jit_solution(17513833814903474328)
XLA Ops:
  0.0 79.7 %shard_map.64 = (bf16[3,2,128,16,128]{4,3,2,1,0:T(8,128)(2,1)S(1)}, bf16[2,2,4,4,4,16,128]{6,5,4,3,2,1,0:T(8,128)(2,1)S(1)}, bf16[18,256,256]{2,1,0:T(8,128)(2,1)S(1)}, bf16[8,2,2,2,32,16,128]{6,5,4,3,2,1,0:T(8,128)(2,1)S(1)}) custom-call(bf16[2,2,4,4,4,64,128]{6,5,4,3,2,1,0:T(8,128)(2,1)} %bitcast.3, f32[64,16384]{1,0:T(8,128)} %bitcast.4, ...), custom_call_target="tpu_custom_call" | custom-call | tf_op jit(solution)/shard_map/pallas_call | solution.py:406
  79.7 4.8 %shard_map.65 = bf16[2,128,64,128]{3,2,1,0:T(8,128)(2,1)} custom-call(bf16[3,2,128,16,128]{4,3,2,1,0:T(8,128)(2,1)S(1)} %get-tuple-element.9.done, bf16[2,2,4,4,4,16,128]{6,5,4,3,2,1,0:T(8,128)(2,1)S(1)} %get-tuple-element.10.last, bf16[18,256,256]{2,1,0:T(8,128)(2,1)S(1)} %get-tuple-element.11.mats, ...), custom_call_target="tpu_custom_call" | custom-call | tf_op jit(solution)/shard_map/pallas_call | solution.py:435

commit v5 on v4

--- a/solution.py
+++ b/solution.py
@@ -142,10 +142,10 @@
     return jnp.concatenate(tiles, 0)
 
 
-def combine(evens, odds, masks, mats, level, powers, re, im):
+def combine(evens, odds, masks, mats, level, powers, re, im, source=None):
     pieces = [[[], []], [[], []]]
     for even, odd, mask in zip(evens, odds, masks):
-        for kind, ref in enumerate((re, im)):
+        for kind, ref in enumerate(source or (re, im)):
             a, b = ref[even], ref[odd]
             pieces[0][kind].append(jnp.where(mask, a, b))
             pieces[1][kind].append(jnp.where(mask, b, a))
@@ -179,7 +179,7 @@
             combine([(s, 0, k) for k in ks], [(s, 1, k ^ step) for k in ks], masks, mats, level, powers, re, im)
 
 
-def joint(mats, powers, re, im, put):
+def joint(mats, powers, re, im, put, source=None):
     low = low_lanes()
     for at in range(0, HALVES, SPAN):
         vs = range(at, at + SPAN)
@@ -187,7 +187,7 @@
         evens = [(e, 0, v // 2) for e, v in zip(side, vs)]
         odds = [(1 - e, 1, v // 2) for e, v in zip(side, vs)]
         masks = [jnp.logical_not(low) if e else low for e in side]
-        combine(evens, odds, masks, mats, LEVELS - 1, powers, re, im)
+        combine(evens, odds, masks, mats, LEVELS - 1, powers, re, im, source)
     for at in range(0, HALVES, SPAN):
         vs = range(at, at + SPAN)
         for parity in range(2):
@@ -201,8 +201,8 @@
 
 def kernel(
     weights, travel, interp_real, interp_imag, eval_real, eval_imag,
-    image, last, mats, last_powers,
-    held, coded, angles, reals, imags, er, ei, powers, re, im, send_sem, recv_sem, load_sem,
+    image, mats, re, im, eighth,
+    held, coded, angles, reals, imags, er, ei, powers, send_sem, recv_sem, load_sem,
 ):
     gx, gy = lax.axis_index("gx"), lax.axis_index("gy")
     xh, z, y, u = gx // 4, gx % 4, gy // 4, gy % 4
@@ -280,7 +280,7 @@
                 index = index + (slice(None),) * (4 - len(index))
                 return weights.at[(stream,) + index + (pl.ds(w * ROWS, ROWS),)]
         mine = peer(axis, 0)[0]
-        target = place_of(stage, stream, w).at[part(axis, mine)]
+        target = held.at[(stage, stream, w) + part(axis, mine)]
 
         def send(k):
             at, device = peer(axis, k)
@@ -295,13 +295,8 @@
 
         return send, keep
 
-    def place_of(stage, stream, w):
-        if isinstance(w, int) and (stage, w) == (2, WAVES - 1) and stream != CODES:
-            return last.at[stream]
-        return held.at[stage, stream, w]
-
     def land(stage, stream, w):
-        place = place_of(stage, stream, w)
+        place = held.at[stage, stream, w]
         pltpu.make_async_copy(place, place, recv_sem.at[stage, stream, w]).wait()
 
     go(2, 0)
@@ -334,24 +329,32 @@
     go(2, 1)
     go(3, 1)
 
+    def slot_of(w):
+        return w - (w + 2) // 3
+
+    def sent(group, stage):
+        for place, (stream, w) in enumerate(GROUPED[group]):
+            blocks = GROUPS - GROUPS // count(axis_of(place, stage))
+            bytes_of = image.at[0, 0, pl.ds(0, blocks)]
+            pltpu.make_async_copy(bytes_of, bytes_of, send_sem.at[stage, stream, w]).wait()
+
     def tabulate(w):
         land(2, CODES, w)
-        place = last_powers if w == WAVES - 1 else powers.at[w // 2]
-        tables(lambda blk, y, u: held[2, CODES, w, blk // 4, blk % 4, y, u], place)
+        tables(lambda blk, y, u: held[2, CODES, w, blk // 4, blk % 4, y, u], powers.at[slot_of(w)])
 
     tabulate(0)
 
     def link(n, _):
         s, w = n % 2, n // 2
         land(2, s, w)
-        chain(s, lambda xz, y, u: held[2, s, w, xz // 4, xz % 4, y, u], mats, powers.at[w // 2], re, im)
-
-        @pl.when(s == 1)
+        chain(s, lambda xz, y, u: held[2, s, w, xz // 4, xz % 4, y, u], mats, powers.at[slot_of(w)], re, im)
+
+        @pl.when((s == 1) & (w < WAVES - 1))
         def _():
             def put(c, d, value):
                 image[w, c, d] = value
 
-            joint(mats, powers.at[w // 2], re, im, put)
+            joint(mats, powers.at[slot_of(w)], re, im, put)
 
         @pl.when(n == 1)
         def _():
@@ -360,38 +363,42 @@
             tabulate(2)
             go(3, 2)
             tabulate(3)
+            for i in range(2):
+                for side in range(2):
+                    for parity in range(2):
+                        eighth[i, side, parity] = powers[slot_of(3), LEVELS - 1, i, side, parity]
+            for stage in range(2):
+                for group in range(4):
+                    sent(group, stage)
+            sent(0, 2)
+            sent(1, 2)
 
         return 0
 
-    lax.fori_loop(0, 2 * (WAVES - 1), link, 0)
-    land(2, 0, WAVES - 1)
-    land(2, 1, WAVES - 1)
-
-    for items in GROUPED:
-        for place, (stream, w) in enumerate(items):
-            for stage in range(3):
-                sent = GROUPS - GROUPS // count(axis_of(place, stage))
-                bytes_of = image.at[0, 0, pl.ds(0, sent)]
-                pltpu.make_async_copy(bytes_of, bytes_of, send_sem.at[stage, stream, w]).wait()
-
-
-def finish(done, last, mats, powers, image, re, im, staged, out_sem):
+    lax.fori_loop(0, 2 * WAVES, link, 0)
+    sent(2, 2)
+    sent(3, 2)
+
+
+class Last:
+    def __init__(self, ref):
+        self.ref = ref
+
+    def __getitem__(self, key):
+        return self.ref[key[1:]]
+
+
+def finish(done, mats, re_in, im_in, eighth, image, re, im, staged, out_sem):
     def out(source, w):
         return pltpu.make_async_copy(source, image.at[:, :, pl.ds(w * ROWS, ROWS)], out_sem.at[w])
 
     for w in range(WAVES - 1):
         out(done.at[w], w).start()
 
-    def side(s, _):
-        chain(s, lambda xz, y, u: last[s, xz // 4, xz % 4, y, u], mats, powers, re, im)
-        return 0
-
-    lax.fori_loop(0, 2, side, 0)
-
     def put(c, d, value):
         staged[c, d] = value
 
-    joint(mats, powers, re, im, put)
+    joint(mats, Last(eighth), re, im, put, (re_in, im_in))
     out(staged, WAVES - 1).start()
     for w in range(WAVES - 1):
         out(done.at[w], w).wait()
@@ -406,12 +413,13 @@
     passed = pl.pallas_call(
         kernel,
         in_specs=[pl.BlockSpec(memory_space=pl.ANY)] * 6,
-        out_specs=[pl.BlockSpec(memory_space=pltpu.VMEM)] * 4,
+        out_specs=[pl.BlockSpec(memory_space=pltpu.VMEM)] * 5,
         out_shape=[
             pltpu.VMEM((WAVES - 1, 2, GROUPS, ROWS, LANES), bf16),
-            pltpu.VMEM((2,) + DIGITS + (ROWS, LANES), bf16),
             pltpu.VMEM((2 * LEVELS + 2, 2 * LANES, 2 * LANES), bf16),
-            pltpu.VMEM((LEVELS, 2) + tiles, bf16),
+            pltpu.VMEM(tiles, bf16),
+            pltpu.VMEM(tiles, bf16),
+            pltpu.VMEM((2,) + tiles, bf16),
         ],
         scratch_shapes=[
             pltpu.VMEM((3, 3, WAVES) + DIGITS + (ROWS, LANES), bf16),
@@ -421,20 +429,18 @@
             pltpu.VMEM(interp_imag.shape, bf16),
             pltpu.VMEM(eval_real.shape, bf16),
             pltpu.VMEM(eval_imag.shape, bf16),
-            pltpu.VMEM((2, LEVELS, 2) + tiles, bf16),
-            pltpu.VMEM(tiles, bf16),
-            pltpu.VMEM(tiles, bf16),
+            pltpu.VMEM((3, LEVELS, 2) + tiles, bf16),
             pltpu.SemaphoreType.DMA((3, 3, WAVES)),
             pltpu.SemaphoreType.DMA((3, 3, WAVES)),
             pltpu.SemaphoreType.DMA((6,)),
         ],
         compiler_params=pltpu.CompilerParams(
-            collective_id=0, has_side_effects=True, vmem_limit_bytes=45 << 20
+            collective_id=0, has_side_effects=True, vmem_limit_bytes=51 << 20
         ),
     )(weights.reshape((2,) + DIGITS + (block_rows, width)), travel.T, interp_real, interp_imag, eval_real, eval_imag)
     image = pl.pallas_call(
         finish,
-        in_specs=[pl.BlockSpec(memory_space=pltpu.VMEM)] * 4,
+        in_specs=[pl.BlockSpec(memory_space=pltpu.VMEM)] * 5,
         out_specs=pl.BlockSpec(memory_space=pl.ANY),
         out_shape=pltpu.HBM((2, GROUPS, block_rows, width), bf16),
         scratch_shapes=[

time: 84.8 us -> 85.4 us (level)
    pallas_call x1, Pallas kernels: 79.7 us -> 82.7 us  [local(): pl.pallas_call(kernel, in_specs=[pl.BlockSpec(memory_space=pl.ANY)] * 6,...]
    pallas_call x1, Pallas kernels: 4.85 us -> 2.39 us  [local(): pl.pallas_call(finish, in_specs=[pl.BlockSpec(memory_space=pltpu.VMEM)] *...]
where the time goes in v5:
time: 85.4 us; the launch traced here: 85.1 us
  Pallas kernels  85.1 us (100%)
    pallas_call x1, Pallas kernels, local(): pl.pallas_call(kernel, in_specs=[pl.BlockSpec(memory_space=pl.ANY)] * 6,...  82.7 us
    pallas_call x1, Pallas kernels, local(): pl.pallas_call(finish, in_specs=[pl.BlockSpec(memory_space=pltpu.VMEM)] *...  2.39 us

profile of v5, /device:TPU:1, one launch (start us, length us, event | category | flops | bytes accessed | tf_op | source)
XLA Modules:
  0.0 85.1 jit_solution(10578401023765535830)
XLA Ops:
  0.0 82.7 %shard_map.64 = (bf16[3,2,128,16,128]{4,3,2,1,0:T(8,128)(2,1)S(1)}, bf16[18,256,256]{2,1,0:T(8,128)(2,1)S(1)}, bf16[2,2,32,16,128]{4,3,2,1,0:T(8,128)(2,1)S(1)},...) custom-call(bf16[2,2,4,4,4,64,128]{6,5,4,3,2,1,0:T(8,128)(2,1)} %bitcast.3, ...), custom_call_target="tpu_custom_call" | custom-call | tf_op jit(solution)/shard_map/pallas_call | solution.py:413
  82.8 2.4 %shard_map.65 = bf16[2,128,64,128]{3,2,1,0:T(8,128)(2,1)} custom-call(bf16[3,2,128,16,128]{4,3,2,1,0:T(8,128)(2,1)S(1)} %get-tuple-element.10.done, bf16[18,256,256]{2,1,0:T(8,128)(2,1)S(1)} %get-tuple-element.11.mats, bf16[2,2,32,16,128]{4,3,2,1,0:T(8,128)(2,1)S(1)} %get-tuple-element.12.re_in, bf16[2,2,32,16,128]{4,3,2,1,0:T(8,128)(2,1)S(1)} %get-tuple-element.13.im_in, ...), custom_call_target="tpu_custom_call" | custom-call | tf_op jit(solution)/shard_map/pallas_call | solution.py:441

commit v6 on v4

--- a/solution.py
+++ b/solution.py
@@ -13,7 +13,7 @@
 WAVES = 4
 LANES = 128
 HALF = LANES // 2
-SPAN = 16
+SPAN = 32
 SCALE = 40.0
 DECODE = 0.018033688011112043
 DIGITS = (2, 4, 4, 4)
@@ -334,6 +334,12 @@
     go(2, 1)
     go(3, 1)
 
+    def sent(group, stage):
+        for place, (stream, w) in enumerate(GROUPED[group]):
+            blocks = GROUPS - GROUPS // count(axis_of(place, stage))
+            bytes_of = image.at[0, 0, pl.ds(0, blocks)]
+            pltpu.make_async_copy(bytes_of, bytes_of, send_sem.at[stage, stream, w]).wait()
+
     def tabulate(w):
         land(2, CODES, w)
         place = last_powers if w == WAVES - 1 else powers.at[w // 2]
@@ -360,19 +366,19 @@
             tabulate(2)
             go(3, 2)
             tabulate(3)
+            for stage in range(2):
+                for group in range(4):
+                    sent(group, stage)
+            sent(0, 2)
+            sent(1, 2)
 
         return 0
 
     lax.fori_loop(0, 2 * (WAVES - 1), link, 0)
     land(2, 0, WAVES - 1)
     land(2, 1, WAVES - 1)
-
-    for items in GROUPED:
-        for place, (stream, w) in enumerate(items):
-            for stage in range(3):
-                sent = GROUPS - GROUPS // count(axis_of(place, stage))
-                bytes_of = image.at[0, 0, pl.ds(0, sent)]
-                pltpu.make_async_copy(bytes_of, bytes_of, send_sem.at[stage, stream, w]).wait()
+    sent(2, 2)
+    sent(3, 2)
 
 
 def finish(done, last, mats, powers, image, re, im, staged, out_sem):

time: 84.8 us -> 84.6 us (level)
  no operation moved by 1% of the time
where the time goes in v6:
time: 84.6 us; the launch traced here: 84.4 us
  Pallas kernels  84.4 us (100%)
    pallas_call x1, Pallas kernels, local(): pl.pallas_call(kernel, in_specs=[pl.BlockSpec(memory_space=pl.ANY)] * 6,...  79.6 us
    pallas_call x1, Pallas kernels, local(): pl.pallas_call(finish, in_specs=[pl.BlockSpec(memory_space=pltpu.VMEM)] *...  4.8 us

profile of v6, /device:TPU:1, one launch (start us, length us, event | category | flops | bytes accessed | tf_op | source)
XLA Modules:
  0.0 84.4 jit_solution(11949384554146167456)
XLA Ops:
  0.0 79.6 %shard_map.64 = (bf16[3,2,128,16,128]{4,3,2,1,0:T(8,128)(2,1)S(1)}, bf16[2,2,4,4,4,16,128]{6,5,4,3,2,1,0:T(8,128)(2,1)S(1)}, bf16[18,256,256]{2,1,0:T(8,128)(2,1)S(1)}, bf16[8,2,2,2,32,16,128]{6,5,4,3,2,1,0:T(8,128)(2,1)S(1)}) custom-call(bf16[2,2,4,4,4,64,128]{6,5,4,3,2,1,0:T(8,128)(2,1)} %bitcast.3, f32[64,16384]{1,0:T(8,128)} %bitcast.4, ...), custom_call_target="tpu_custom_call" | custom-call | tf_op jit(solution)/shard_map/pallas_call | solution.py:412
  79.6 4.8 %shard_map.65 = bf16[2,128,64,128]{3,2,1,0:T(8,128)(2,1)} custom-call(bf16[3,2,128,16,128]{4,3,2,1,0:T(8,128)(2,1)S(1)} %get-tuple-element.9.done, bf16[2,2,4,4,4,16,128]{6,5,4,3,2,1,0:T(8,128)(2,1)S(1)} %get-tuple-element.10.last, bf16[18,256,256]{2,1,0:T(8,128)(2,1)S(1)} %get-tuple-element.11.mats, ...), custom_call_target="tpu_custom_call" | custom-call | tf_op jit(solution)/shard_map/pallas_call | solution.py:441
